TPU v7x, 32 devices: a whole 2x2x4 slice. The times are simulated.
32 devices in a mesh: seq: 16 (over z, y, core), tp: 2 (over x).
Axes of the slice: x: 2, y: 2, z: 4, core: 2. Of those that a mesh axis runs over, the one named last changes fastest.
Arguments:
- tokens: bfloat16 [4096, 4096], P('seq', 'tp'), may hold values from -6 to 6
- ln_gain: float32 [4096], replicated, may hold values from 0.1 to 1.9
- ln_bias: float32 [4096], replicated, may hold values from -3 to 3
- w_qkv: bfloat16 [4096, 16, 3, 128], P('seq', 'tp'), may hold values from -3 to 3
- w_out: bfloat16 [16, 128, 4096], P('tp', None, 'seq'), may hold values from -0.25 to 0.25
- layer_scale: float32 [4096], P('tp'), may hold values from 0.5 to 2
- grids: int32 [2], replicated, may hold values from 24 to 40, as said below
- offsets: int32 [3], replicated, may hold values from 0 to 2186, as said below
Outputs:
- merged: bfloat16 [4096, 4, 4096], P('seq', None, 'tp')
Inputs may be any that keep to these rules, and one draw needn't show every extreme that they name: `grids`: every side is even and some image has side exactly 40. Of images 2k and 2k + 1, one side is drawn and the other is the largest even side of at most 40 whose square keeps the two squares' sum within 2176. offsets[0] = 0 and offsets[s + 1] = offsets[s] + 5 + grids[s] * grids[s].
All inputs are finite; a program needn't handle non-finite values.
Results may differ from a plain program's by a relative error of at most 0.015.
Values may be sent and summed in bfloat16 or wider, within the bound.
A program may use at most 128 MiB of HBM per device.

v0:
```python
import math

import jax
import jax.numpy as jnp
from jax import lax
from jax.sharding import PartitionSpec as P

HALO = 48
REACH = 7


def from_behind(shard, axis, by):
    count = lax.axis_size(axis)
    pairs = [(i, i + by) for i in range(count) if 0 <= i + by < count]
    return lax.ppermute(shard, axis, pairs)


def layout_rows(row_ids, offsets, grids, row_count):
    images = grids.shape[0]
    image_ends = offsets[1:]
    segment = jnp.sum((row_ids[:, None] >= image_ends[None, :]).astype(jnp.int32), axis=1)
    inside = (row_ids >= 0) & (row_ids < row_count) & (segment < images)
    onehot = (
        jnp.minimum(segment, images - 1)[:, None] == jnp.arange(images, dtype=jnp.int32)[None, :]
    ).astype(jnp.int32)
    image_start = jnp.sum(onehot * offsets[None, :-1], axis=1)
    grid_side = jnp.sum(onehot * grids[None, :], axis=1)
    position = row_ids - image_start
    is_patch = inside & (position >= 5)
    patch_index = jnp.maximum(position - 5, 0)
    return (segment, inside, is_patch, patch_index // grid_side, patch_index % grid_side, grid_side)


def rotate(vectors, is_patch, grid_row, grid_col, grid_side):
    quarter = vectors.shape[-1] // 4
    frequency = 2.0 * math.pi * jnp.power(100.0, -jnp.arange(quarter, dtype=jnp.float32) / quarter)
    side_float = grid_side.astype(jnp.float32)
    coord_row = (2 * grid_row + 1).astype(jnp.float32) / side_float - 1.0
    coord_col = (2 * grid_col + 1).astype(jnp.float32) / side_float - 1.0
    angles_row = jnp.where(is_patch[:, None], coord_row[:, None] * frequency[None, :], 0.0)
    angles_col = jnp.where(is_patch[:, None], coord_col[:, None] * frequency[None, :], 0.0)

    def rotate_half(block_vals, angles):
        first_half = block_vals[..., :quarter]
        second_half = block_vals[..., quarter:]
        cosine = jnp.cos(angles)[:, None, :]
        sine_part = jnp.sin(angles)[:, None, :]
        return jnp.concatenate(
            [
                first_half * cosine - second_half * sine_part,
                second_half * cosine + first_half * sine_part,
            ],
            axis=-1,
        )

    return jnp.concatenate(
        [
            rotate_half(vectors[..., : 2 * quarter], angles_row),
            rotate_half(vectors[..., 2 * quarter :], angles_col),
        ],
        axis=-1,
    )


def attend_blocks(query_matrix, kv_blocks, key_segment, key_inside, query_segment, query_inside):
    logit_scale_factor = 1.0 / math.sqrt(query_matrix.shape[-1])
    rows_here = query_matrix.shape[0]
    heads_here = query_matrix.shape[1]

    def block_scores(block_of_keys, segment_block, inside_block):
        attention_logits = (
            jnp.einsum(
                "ecn,dcn->ced", query_matrix, block_of_keys, preferred_element_type=jnp.float32
            )
            * logit_scale_factor
        )
        allowed = (
            query_inside[:, None]
            & inside_block[None, :]
            & (query_segment[:, None] == segment_block[None, :])
        )
        return (jnp.where(allowed[None], attention_logits, -1e30), allowed)

    def max_step(carry, input_block_rows):
        row_max, row_total = carry
        masked, allowed = block_scores(
            input_block_rows[0][:, 0], input_block_rows[1], input_block_rows[2]
        )
        new_max = jnp.maximum(row_max, jnp.max(masked, axis=2, keepdims=True))
        exp_terms = jnp.where(allowed[None], jnp.exp(masked - new_max), 0.0)
        row_total = row_total * jnp.exp(row_max - new_max) + jnp.sum(
            exp_terms, axis=2, keepdims=True
        )
        return ((new_max, row_total), None)

    start_max = jnp.full((heads_here, rows_here, 1), -1e30, jnp.float32)
    start_total = jnp.zeros((heads_here, rows_here, 1), jnp.float32)
    (row_max, row_total), _ = lax.scan(
        max_step, (start_max, start_total), (kv_blocks, key_segment, key_inside)
    )
    row_total = jnp.where(query_inside[None, :, None], row_total, 1.0)

    def sum_step(running, input_block_rows):
        masked, allowed = block_scores(
            input_block_rows[0][:, 0], input_block_rows[1], input_block_rows[2]
        )
        exp_terms = jnp.where(allowed[None], jnp.exp(masked - row_max), 0.0)
        softmax_probabilities = (exp_terms / row_total).astype(jnp.bfloat16)
        return (
            running
            + jnp.einsum(
                "vgm,mvb->gvb",
                softmax_probabilities,
                input_block_rows[0][:, 1],
                preferred_element_type=jnp.float32,
            ),
            None,
        )

    start_sum = jnp.zeros((rows_here, heads_here, query_matrix.shape[2]), jnp.float32)
    attended_output, _ = lax.scan(sum_step, start_sum, (kv_blocks, key_segment, key_inside))
    attended_output = jnp.where(query_inside[:, None, None], attended_output, 0.0)
    return attended_output.astype(jnp.bfloat16)


def body(tokens, ln_gain, ln_bias, w_qkv, w_out, layer_scale, grids, offsets):
    rows_here = tokens.shape[0]
    row_count = rows_here * lax.axis_size("seq")
    first_row = lax.axis_index("seq") * rows_here
    gathered = lax.all_gather(tokens, "tp", axis=1, tiled=True)
    widened = gathered.astype(jnp.float32)
    average = jnp.mean(widened, axis=-1, keepdims=True)
    spread_sq = jnp.mean(jnp.square(widened - average), axis=-1, keepdims=True)
    normed = ((widened - average) * lax.rsqrt(spread_sq + 1e-06) * ln_gain + ln_bias).astype(
        jnp.bfloat16
    )
    qkv_sums = jnp.einsum(
        "td,dhcf->thcf",
        normed,
        lax.all_gather(w_qkv, "seq", axis=0, tiled=True),
        preferred_element_type=jnp.float32,
    )
    row_ids = first_row + jnp.arange(rows_here, dtype=jnp.int32)
    segment, inside, is_patch, grid_row, grid_col, grid_side = layout_rows(
        row_ids, offsets, grids, row_count
    )
    query_matrix = rotate(qkv_sums[:, :, 0], is_patch, grid_row, grid_col, grid_side).astype(
        jnp.bfloat16
    )
    roped_keys = rotate(qkv_sums[:, :, 1], is_patch, grid_row, grid_col, grid_side).astype(
        jnp.bfloat16
    )
    values = qkv_sums[:, :, 2].astype(jnp.bfloat16)
    key_value = jnp.stack([roped_keys, values], axis=1)
    block_count = 2 * REACH + 1
    pieces = []
    for block_slot in range(block_count):
        distance = REACH - block_slot
        if distance == 0:
            pieces.append(key_value)
        else:
            pieces.append(from_behind(key_value, "seq", distance))
    kv_blocks = jnp.stack(pieces, axis=0)
    key_rows = first_row - REACH * rows_here + jnp.arange(block_count * rows_here, dtype=jnp.int32)
    key_layout = layout_rows(key_rows, offsets, grids, row_count)
    key_segment = key_layout[0].reshape(block_count, rows_here)
    key_inside = key_layout[1].reshape(block_count, rows_here)
    attended_output = attend_blocks(
        query_matrix, kv_blocks, key_segment, key_inside, segment, inside
    )
    projected = jnp.einsum(
        "thf,hfc->tc",
        attended_output,
        lax.all_gather(w_out, "seq", axis=2, tiled=True),
        preferred_element_type=jnp.float32,
    )
    head_share = lax.psum_scatter(
        projected.astype(jnp.bfloat16), "tp", scatter_dimension=1, tiled=True
    ).astype(jnp.float32)
    layer_out = (tokens.astype(jnp.float32) + layer_scale * head_share).astype(jnp.bfloat16)
    next_rows = from_behind(layer_out[:HALO], "seq", -1)
    extended = jnp.concatenate([layer_out, next_rows], axis=0)
    is_corner = is_patch & (grid_row % 2 == 0) & (grid_col % 2 == 0)
    local_ids = jnp.arange(rows_here, dtype=jnp.int32)
    corner_index = jnp.stack(
        [local_ids, local_ids + 1, local_ids + grid_side, local_ids + grid_side + 1], axis=1
    )
    corner_index = jnp.clip(corner_index, 0, extended.shape[0] - 1)
    merged = jnp.take(extended, corner_index, axis=0)
    return jnp.where(is_corner[:, None, None], merged, jnp.zeros_like(merged))


def solution(mesh):
    placed = (
        P("seq", "tp"),
        P(),
        P(),
        P("seq", "tp", None, None),
        P("tp", None, "seq"),
        P("tp"),
        P(),
        P(),
    )
    return jax.shard_map(
        body, mesh=mesh, in_specs=placed, out_specs=P("seq", None, "tp"), check_vma=False
    )
```

profile of v0, /device:TPU:5, one launch (start us, length us, event | category | flops | bytes accessed | tf_op | source)
XLA Modules:
  0.0 794.7 jit_solution(16746168037247728200)
XLA Ops:
  11.0 32.3 %all-gather.4.cloned.1.call-done = bf16[256,4096]{1,0:T(8,128)(2,1)} async-done(((bf16[256,2048]{1,0:T(8,128)(2,1)}), bf16[256,4096]{1,0:T(8,128)(2,1)}) %all-gather.4.cloned.1.call-update) | async-done | bytes 2097168 | tf_op jit(solution)/shard_map/all_gather | solution.py:130
  47.7 134.5 %all-gather.6.cloned.1.call-done = bf16[4096,8,3,128]{0,3,2,1:T(8,128)(2,1)} async-done(((bf16[256,8,3,128]{0,3,2,1:T(8,128)(2,1)}), bf16[4096,8,3,128]{0,3,2,1:T(8,128)(2,1)}) %all-gather.6.cloned.1.call-update) | async-done | bytes 25165840 | tf_op jit(solution)/shard_map/all_gather | solution.py:140
  182.2 12.2 %fusion.24 = f32[256,3072]{0,1:S(1)} fusion(bf16[4096,3072]{0,1:T(8,128)(2,1)} %bitcast.158, bf16[256,4096]{1,0:T(8,128)(2,1)S(1)} %copy-done, f32[4096]{0:T(1024)S(1)} %copy-done.5, f32[4096]{0:T(1024)S(1)} %copy-done.6, f32[256]{0:T(256)S(1)} %add_rsqrt_fusion, f32[256]{0:T(256)S(1)} %broadcast_multiply_fusion), kind=kOutput, calls=%fused_computation.47 | convolution fusion | flops 6448742400 | bytes 30443520
  210.1 26.1 %collective-permute-done = bf16[256,2,8,128]{0,3,2,1:T(8,128)(2,1)} collective-permute-done((bf16[256,2,8,128]{0,3,2,1:T(8,128)(2,1)}, bf16[256,2,8,128]{0,3,2,1:T(8,128)(2,1)}, u32[]{:S(2)}, u32[]{:S(2)}) %collective-permute-start) | collective-permute-done | bytes 1048608 | tf_op jit(solution)/shard_map/ppermute | solution.py:15
  236.2 15.6 %collective-permute-start.5 = (bf16[256,2,8,128]{0,3,2,1:T(8,128)(2,1)}, bf16[256,2,8,128]{0,3,2,1:T(8,128)(2,1)S(1)}, u32[]{:S(2)}, u32[]{:S(2)}) collective-permute-start(bf16[256,2,8,128]{0,3,2,1:T(8,128)(2,1)} %pad_maximum_fusion.1), channel_id=1, source_target_pairs={{0,4},{2,6},{4,8},{6,10},{8,12},{10,14},{12,16},{14,18},{16,20},{1... | collective-permute-start | bytes 3145736 | tf_op jit(solution)/shard_map/ppermute | solution.py:15
  254.2 7.1 collective-permute-done.1
  261.2 53.9 %collective-permute-start.6 = (bf16[256,2,8,128]{0,3,2,1:T(8,128)(2,1)}, bf16[256,2,8,128]{0,3,2,1:T(8,128)(2,1)S(1)}, u32[]{:S(2)}, u32[]{:S(2)}) collective-permute-start(bf16[256,2,8,128]{0,3,2,1:T(8,128)(2,1)} %pad_maximum_fusion.1), channel_id=1, source_target_pairs={{0,2},{2,4},{4,6},{6,8},{8,10},{10,12},{12,14},{14,16},{16,18},{18... | collective-permute-start | bytes 3145736 | tf_op jit(solution)/shard_map/ppermute | solution.py:15
  321.7 4.3 collective-permute-done.3
  330.1 32.2 %collective-permute-done.4 = bf16[256,2,8,128]{0,3,2,1:T(8,128)(2,1)} collective-permute-done((bf16[256,2,8,128]{0,3,2,1:T(8,128)(2,1)}, bf16[256,2,8,128]{0,3,2,1:T(8,128)(2,1)}, u32[]{:S(2)}, u32[]{:S(2)}) %collective-permute-start.4) | collective-permute-done | bytes 1048608 | tf_op jit(solution)/shard_map/ppermute | solution.py:15
  366.6 18.3 %collective-permute-done.5 = bf16[256,2,8,128]{0,3,2,1:T(8,128)(2,1)S(1)} collective-permute-done((bf16[256,2,8,128]{0,3,2,1:T(8,128)(2,1)}, bf16[256,2,8,128]{0,3,2,1:T(8,128)(2,1)S(1)}, u32[]{:S(2)}, u32[]{:S(2)}) %collective-permute-start.5) | collective-permute-done | bytes 1048608 | tf_op jit(solution)/shard_map/ppermute | solution.py:15
  387.2 9.2 %collective-permute-done.6 = bf16[256,2,8,128]{0,3,2,1:T(8,128)(2,1)S(1)} collective-permute-done((bf16[256,2,8,128]{0,3,2,1:T(8,128)(2,1)}, bf16[256,2,8,128]{0,3,2,1:T(8,128)(2,1)S(1)}, u32[]{:S(2)}, u32[]{:S(2)}) %collective-permute-start.6) | collective-permute-done | bytes 1048608 | tf_op jit(solution)/shard_map/ppermute | solution.py:15
  404.8 29.7 %collective-permute-done.9 = bf16[256,2,8,128]{0,3,2,1:T(8,128)(2,1)S(1)} collective-permute-done((bf16[256,2,8,128]{0,3,2,1:T(8,128)(2,1)}, bf16[256,2,8,128]{0,3,2,1:T(8,128)(2,1)S(1)}, u32[]{:S(2)}, u32[]{:S(2)}) %collective-permute-start.9) | collective-permute-done | bytes 1048608 | tf_op jit(solution)/shard_map/ppermute | solution.py:15
  435.5 30.0 %collective-permute-done.10 = bf16[256,2,8,128]{0,3,2,1:T(8,128)(2,1)S(1)} collective-permute-done((bf16[256,2,8,128]{0,3,2,1:T(8,128)(2,1)}, bf16[256,2,8,128]{0,3,2,1:T(8,128)(2,1)S(1)}, u32[]{:S(2)}, u32[]{:S(2)}) %collective-permute-start.10) | collective-permute-done | bytes 1048608 | tf_op jit(solution)/shard_map/ppermute | solution.py:15
  466.7 83.1 %collective-permute-done.11 = bf16[256,2,8,128]{0,3,2,1:T(8,128)(2,1)S(1)} collective-permute-done((bf16[256,2,8,128]{0,3,2,1:T(8,128)(2,1)}, bf16[256,2,8,128]{0,3,2,1:T(8,128)(2,1)S(1)}, u32[]{:S(2)}, u32[]{:S(2)}) %collective-permute-start.11) | collective-permute-done | bytes 1048608 | tf_op jit(solution)/shard_map/ppermute | solution.py:15
  550.8 18.5 %collective-permute-done.12 = bf16[256,2,8,128]{0,3,2,1:T(8,128)(2,1)S(1)} collective-permute-done((bf16[256,2,8,128]{0,3,2,1:T(8,128)(2,1)}, bf16[256,2,8,128]{0,3,2,1:T(8,128)(2,1)S(1)}, u32[]{:S(2)}, u32[]{:S(2)}) %collective-permute-start.12) | collective-permute-done | bytes 1048608 | tf_op jit(solution)/shard_map/ppermute | solution.py:15
  571.6 20.7 %copy.44 = bf16[15,256,2,8,128]{4,1,3,2,0:T(8,128)(2,1)} copy(bf16[15,256,2,8,128]{1,4,3,2,0:T(8,128)(2,1)} %bitcast_dynamic-update-slice_fusion) | data formatting | bytes 31457280
  592.3 38.3 %while.24 = (s32[]{:T(128)}, f32[8,256,1]{1,0,2:T(8,128)S(1)}, f32[8,256,1]{1,0,2:T(8,128)S(1)}, pred[256]{0:T(512)(128)(4,1)S(1)}, pred[15,256]{1,0:T(8,128)(4,...) while((s32[]{:T(128)}, f32[8,256,1]{1,0,2:T(8,128)S(1)}, ...), condition=%wide.region_9.10_spmd.clone, body=%wide.region_6.9_spmd.clone.sunk | while | flops 138618880 | bytes 7648388 | solution.py:98
  630.6 69.8 %while.25 = (s32[]{:T(128)}, f32[256,8,128]{0,2,1:T(8,128)}, bf16[15,256,2,8,128]{4,1,3,2,0:T(8,128)(2,1)}, pred[256]{0:T(512)(128)(4,1)S(1)}, pred[15,256]{1,0:...) while((s32[]{:T(128)}, f32[256,8,128]{0,2,1:T(8,128)}, ...), condition=%wide.region_11.12_spmd.clone, body=%wide.region_10.11_spmd.clone.sunk | while | flops 272302080 | bytes 5919883 | solution.py:121
  700.5 7.5 fusion.17
  708.5 50.8 %reduce-scatter.2.cloned.1.call-done = bf16[256,2048]{1,0:T(8,128)(2,1)} async-done(((bf16[256,4096]{1,0:T(8,128)(2,1)}), bf16[256,2048]{1,0:T(8,128)(2,1)}) %reduce-scatter.2.cloned.1.call-update) | async-done | bytes 1048592 | tf_op jit(solution)/shard_map/reduce_scatter | solution.py:177
  763.6 5.3 collective-permute-done.14
  768.9 6.0 gather_fusion
  774.9 7.2 reshape.610
  782.1 6.1 select_select_fusion
  (309 shorter events, 169.3 us)
Async XLA Ops:
  6.5 36.7 %all-gather.4.cloned.1.call-start = ((), (), s32[]{:S(2)}) async-start(), calls=%async_computation.1 | async-start | bytes 3145728 | tf_op jit(solution)/shard_map/all_gather | solution.py:130
  7.3 174.9 %copy-start.5 = (f32[4096]{0:T(1024)S(1)}, f32[4096]{0:T(1024)}, u32[]{:S(2)}) copy-start(f32[4096]{0:T(1024)} %param.14) | copy-start | bytes 49156
  7.3 174.9 %copy-start.6 = (f32[4096]{0:T(1024)S(1)}, f32[4096]{0:T(1024)}, u32[]{:S(2)}) copy-start(f32[4096]{0:T(1024)} %param.13) | copy-start | bytes 49156
  7.3 174.9 %all-gather.6.cloned.1.call-start = ((), (), s32[]{:S(2)}) async-start(), calls=%async_computation.2 | async-start | bytes 26738688 | tf_op jit(solution)/shard_map/all_gather | solution.py:140
  10.2 690.3 %all-gather.8.cloned.1.call-start = ((), (), s32[]{:S(2)}) async-start(), calls=%async_computation.3 | async-start | bytes 8912896 | tf_op jit(solution)/shard_map/all_gather | solution.py:174
  43.3 138.9 %copy-start = (bf16[256,4096]{1,0:T(8,128)(2,1)S(1)}, bf16[256,4096]{1,0:T(8,128)(2,1)}, u32[]{:S(2)}) copy-start(bf16[256,4096]{1,0:T(8,128)(2,1)} %all-gather.4.cloned.1.call-done) | copy-start | bytes 6291460
  195.9 40.3 %collective-permute-start = (bf16[256,2,8,128]{0,3,2,1:T(8,128)(2,1)}, bf16[256,2,8,128]{0,3,2,1:T(8,128)(2,1)}, u32[]{:S(2)}, u32[]{:S(2)}) collective-permute-start(bf16[256,2,8,128]{0,3,2,1:T(8,128)(2,1)} %pad_maximum_fusion.1), channel_id=1, source_target_pairs={{0,14},{2,16},{4,18},{6,20},{8,22},{10,24},{12,26},{14,28},{16,30}... | collective-permute-start | bytes 3145736 | tf_op jit(solution)/shard_map/ppermute | solution.py:15
  199.9 559.5 %reduce-scatter.2.cloned.1.call-start = ((), (), s32[]{:S(2)}) async-start(), calls=%async_computation.4 | async-start | bytes 3145728 | tf_op jit(solution)/shard_map/reduce_scatter | solution.py:177
  199.9 61.3 %collective-permute-start.1 = (bf16[256,2,8,128]{0,3,2,1:T(8,128)(2,1)}, bf16[256,2,8,128]{0,3,2,1:T(8,128)(2,1)}, u32[]{:S(2)}, u32[]{:S(2)}) collective-permute-start(bf16[256,2,8,128]{0,3,2,1:T(8,128)(2,1)} %pad_maximum_fusion.1), channel_id=1, source_target_pairs={{0,12},{2,14},{4,16},{6,18},{8,20},{10,22},{12,24},{14,26},{16,28}... | collective-permute-start | bytes 3145736 | tf_op jit(solution)/shard_map/ppermute | solution.py:15
  202.3 115.1 %collective-permute-start.2 = (bf16[256,2,8,128]{0,3,2,1:T(8,128)(2,1)}, bf16[256,2,8,128]{0,3,2,1:T(8,128)(2,1)}, u32[]{:S(2)}, u32[]{:S(2)}) collective-permute-start(bf16[256,2,8,128]{0,3,2,1:T(8,128)(2,1)} %pad_maximum_fusion.1), channel_id=1, source_target_pairs={{0,10},{2,12},{4,14},{6,16},{8,18},{10,20},{12,22},{14,24},{16,26}... | collective-permute-start | bytes 3145736 | tf_op jit(solution)/shard_map/ppermute | solution.py:15
  205.4 120.5 %collective-permute-start.3 = (bf16[256,2,8,128]{0,3,2,1:T(8,128)(2,1)}, bf16[256,2,8,128]{0,3,2,1:T(8,128)(2,1)}, u32[]{:S(2)}, u32[]{:S(2)}) collective-permute-start(bf16[256,2,8,128]{0,3,2,1:T(8,128)(2,1)} %pad_maximum_fusion.1), channel_id=1, source_target_pairs={{0,8},{2,10},{4,12},{6,14},{8,16},{10,18},{12,20},{14,22},{16,24},... | collective-permute-start | bytes 3145736 | tf_op jit(solution)/shard_map/ppermute | solution.py:15
  207.7 154.6 %collective-permute-start.4 = (bf16[256,2,8,128]{0,3,2,1:T(8,128)(2,1)}, bf16[256,2,8,128]{0,3,2,1:T(8,128)(2,1)}, u32[]{:S(2)}, u32[]{:S(2)}) collective-permute-start(bf16[256,2,8,128]{0,3,2,1:T(8,128)(2,1)} %pad_maximum_fusion.1), channel_id=1, source_target_pairs={{0,6},{2,8},{4,10},{6,12},{8,14},{10,16},{12,18},{14,20},{16,22},{... | collective-permute-start | bytes 3145736 | tf_op jit(solution)/shard_map/ppermute | solution.py:15
  236.2 148.6 %collective-permute-start.5 = (bf16[256,2,8,128]{0,3,2,1:T(8,128)(2,1)}, bf16[256,2,8,128]{0,3,2,1:T(8,128)(2,1)S(1)}, u32[]{:S(2)}, u32[]{:S(2)}) collective-permute-start(bf16[256,2,8,128]{0,3,2,1:T(8,128)(2,1)} %pad_maximum_fusion.1), channel_id=1, source_target_pairs={{0,4},{2,6},{4,8},{6,10},{8,12},{10,14},{12,16},{14,18},{16,20},{1... | collective-permute-start | bytes 3145736 | tf_op jit(solution)/shard_map/ppermute | solution.py:15
  261.2 135.2 %collective-permute-start.6 = (bf16[256,2,8,128]{0,3,2,1:T(8,128)(2,1)}, bf16[256,2,8,128]{0,3,2,1:T(8,128)(2,1)S(1)}, u32[]{:S(2)}, u32[]{:S(2)}) collective-permute-start(bf16[256,2,8,128]{0,3,2,1:T(8,128)(2,1)} %pad_maximum_fusion.1), channel_id=1, source_target_pairs={{0,2},{2,4},{4,6},{6,8},{8,10},{10,12},{12,14},{14,16},{16,18},{18... | collective-permute-start | bytes 3145736 | tf_op jit(solution)/shard_map/ppermute | solution.py:15
  317.4 82.4 %collective-permute-start.7 = (bf16[256,2,8,128]{0,3,2,1:T(8,128)(2,1)}, bf16[256,2,8,128]{0,3,2,1:T(8,128)(2,1)S(1)}, u32[]{:S(2)}, u32[]{:S(2)}) collective-permute-start(bf16[256,2,8,128]{0,3,2,1:T(8,128)(2,1)} %pad_maximum_fusion.1), channel_id=1, source_target_pairs={{2,0},{4,2},{6,4},{8,6},{10,8},{12,10},{14,12},{16,14},{18,16},{20... | collective-permute-start | bytes 3145736 | tf_op jit(solution)/shard_map/ppermute | solution.py:15
  325.9 76.3 %collective-permute-start.8 = (bf16[256,2,8,128]{0,3,2,1:T(8,128)(2,1)}, bf16[256,2,8,128]{0,3,2,1:T(8,128)(2,1)S(1)}, u32[]{:S(2)}, u32[]{:S(2)}) collective-permute-start(bf16[256,2,8,128]{0,3,2,1:T(8,128)(2,1)} %pad_maximum_fusion.1), channel_id=1, source_target_pairs={{4,0},{6,2},{8,4},{10,6},{12,8},{14,10},{16,12},{18,14},{20,16},{2... | collective-permute-start | bytes 3145736 | tf_op jit(solution)/shard_map/ppermute | solution.py:15
  362.3 72.2 %collective-permute-start.9 = (bf16[256,2,8,128]{0,3,2,1:T(8,128)(2,1)}, bf16[256,2,8,128]{0,3,2,1:T(8,128)(2,1)S(1)}, u32[]{:S(2)}, u32[]{:S(2)}) collective-permute-start(bf16[256,2,8,128]{0,3,2,1:T(8,128)(2,1)} %pad_maximum_fusion.1), channel_id=1, source_target_pairs={{6,0},{8,2},{10,4},{12,6},{14,8},{16,10},{18,12},{20,14},{22,16},{... | collective-permute-start | bytes 3145736 | tf_op jit(solution)/shard_map/ppermute | solution.py:15
  384.8 80.7 %collective-permute-start.10 = (bf16[256,2,8,128]{0,3,2,1:T(8,128)(2,1)}, bf16[256,2,8,128]{0,3,2,1:T(8,128)(2,1)S(1)}, u32[]{:S(2)}, u32[]{:S(2)}) collective-permute-start(bf16[256,2,8,128]{0,3,2,1:T(8,128)(2,1)} %pad_maximum_fusion.1), channel_id=1, source_target_pairs={{8,0},{10,2},{12,4},{14,6},{16,8},{18,10},{20,12},{22,14},{24,16},... | collective-permute-start | bytes 3145736 | tf_op jit(solution)/shard_map/ppermute | solution.py:15
  396.4 153.3 %collective-permute-start.11 = (bf16[256,2,8,128]{0,3,2,1:T(8,128)(2,1)}, bf16[256,2,8,128]{0,3,2,1:T(8,128)(2,1)S(1)}, u32[]{:S(2)}, u32[]{:S(2)}) collective-permute-start(bf16[256,2,8,128]{0,3,2,1:T(8,128)(2,1)} %pad_maximum_fusion.1), channel_id=1, source_target_pairs={{10,0},{12,2},{14,4},{16,6},{18,8},{20,10},{22,12},{24,14},{26,16}... | collective-permute-start | bytes 3145736 | tf_op jit(solution)/shard_map/ppermute | solution.py:15
  399.8 169.5 %collective-permute-start.12 = (bf16[256,2,8,128]{0,3,2,1:T(8,128)(2,1)}, bf16[256,2,8,128]{0,3,2,1:T(8,128)(2,1)S(1)}, u32[]{:S(2)}, u32[]{:S(2)}) collective-permute-start(bf16[256,2,8,128]{0,3,2,1:T(8,128)(2,1)} %pad_maximum_fusion.1), channel_id=1, source_target_pairs={{12,0},{14,2},{16,4},{18,6},{20,8},{22,10},{24,12},{26,14},{28,16}... | collective-permute-start | bytes 3145736 | tf_op jit(solution)/shard_map/ppermute | solution.py:15
  402.2 168.3 %collective-permute-start.13 = (bf16[256,2,8,128]{0,3,2,1:T(8,128)(2,1)}, bf16[256,2,8,128]{0,3,2,1:T(8,128)(2,1)S(1)}, u32[]{:S(2)}, u32[]{:S(2)}) collective-permute-start(bf16[256,2,8,128]{0,3,2,1:T(8,128)(2,1)} %pad_maximum_fusion.1), channel_id=1, source_target_pairs={{14,0},{16,2},{18,4},{20,6},{22,8},{24,10},{26,12},{28,14},{30,16}... | collective-permute-start | bytes 3145736 | tf_op jit(solution)/shard_map/ppermute | solution.py:15
  700.5 58.8 %copy-start.1 = (bf16[256,2048]{1,0:T(8,128)(2,1)S(1)}, bf16[256,2048]{1,0:T(8,128)(2,1)}, u32[]{:S(2)}) copy-start(bf16[256,2048]{1,0:T(8,128)(2,1)} %param.12) | copy-start | bytes 3145732
  700.5 58.8 %copy-start.2 = (f32[2048]{0:T(1024)S(1)}, f32[2048]{0:T(1024)}, u32[]{:S(2)}) copy-start(f32[2048]{0:T(1024)} %param.17) | copy-start | bytes 24580
  761.0 7.9 collective-permute-start.14
  (2 other events, 7.6 us)
Sparse Core Ops, SparseCore 0:
  8.9 34.3 all-gather.3
  44.8 137.3 all-gather.5
  200.0 153.7 all-gather.7
  708.1 51.1 reduce-scatter.1
where the time goes:
time: 798 us; the launch traced here: 795 us
  waiting for transfers between devices  482 us (60%)
  local copies, waits for them, and re-layouts  99.3 us (12%)
  starting transfers between devices  96.7 us (12%)
  matrix products  74.1 us (9%)
  other arithmetic  27.6 us (3%)
  between operations  13.5 us (2%)
    ppermute x15, waiting for transfers between devices, from_behind(): return lax.ppermute(shard, axis, pairs)  264 us
    all_gather x1, waiting for transfers between devices, body(): lax.all_gather(w_qkv, 'seq', axis=0, tiled=True)  134 us
    ppermute x15, starting transfers between devices, from_behind(): return lax.ppermute(shard, axis, pairs)  96.6 us
    reduce_scatter x1, waiting for transfers between devices, body(): lax.psum_scatter(projected.astype(jnp.bfloat16), 'tp', scatter_dimension=...  50.8 us
    dot_general x15, matrix products, sum_step(): jnp.einsum('vgm,mvb->gvb', softmax_probabilities, input_block_rows[0][:,...  47.4 us
    unnamed x31, local copies, waits for them, and re-layouts  44.1 us
    squeeze x30, local copies, waits for them, and re-layouts, attend_blocks(): lax.scan(max_step, (start_max, start_total), (kv_blocks, key_segment, key...  39 us
    all_gather x1, waiting for transfers between devices, body(): gathered = lax.all_gather(tokens, 'tp', axis=1, tiled=True)  32.3 us
  transfers between devices with their start and end apart: 19, of which 14 were waited for; matrix products, arithmetic and copies ran while one was open for 20% of the time, Pallas kernels for 0%

commit v1 on v0

--- a/solution.py
+++ b/solution.py
@@ -3,6 +3,8 @@
 import jax
 import jax.numpy as jnp
 from jax import lax
+from jax.experimental import pallas as pl
+from jax.experimental.pallas import tpu as pltpu
 from jax.sharding import PartitionSpec as P
 
 HALO = 48
@@ -123,7 +125,7 @@
     return attended_output.astype(jnp.bfloat16)
 
 
-def body(tokens, ln_gain, ln_bias, w_qkv, w_out, layer_scale, grids, offsets):
+def window_body(tokens, ln_gain, ln_bias, w_qkv, w_out, layer_scale, grids, offsets):
     rows_here = tokens.shape[0]
     row_count = rows_here * lax.axis_size("seq")
     first_row = lax.axis_index("seq") * rows_here
@@ -190,6 +192,354 @@
     return jnp.where(is_corner[:, None, None], merged, jnp.zeros_like(merged))
 
 
+PAIR_ROWS = 24 * 24 + 40 * 40 + 10
+MESH = pl.DeviceIdType.MESH
+
+
+def greet(seq, s, t, across):
+    barrier = pltpu.get_barrier_semaphore()
+
+    @pl.loop(1, seq)
+    def _(i):
+        pl.semaphore_signal(
+            barrier, inc=1, device_id=(lax.rem(s + i, seq), t), device_id_type=MESH
+        )
+
+    if across:
+        pl.semaphore_signal(barrier, inc=1, device_id=(s, 1 - t), device_id_type=MESH)
+    pl.semaphore_wait(barrier, seq - 1 + across)
+
+
+def gather_kernel(
+    seq, tail, tok_ref, w_ref, x_ref, wg_ref, own_sem, tsend, trecv, wown, wsend, wrecv, fsend, frecv
+):
+    s = lax.axis_index("seq")
+    t = lax.axis_index("tp")
+    z, y, c = s // 4, (s // 2) % 2, s % 2
+    y_side = s + 2 - 4 * y
+    core_side = s + 1 - 2 * c
+    rows, width = tok_ref.shape
+    half_width = width // 2
+    pairs = seq // 2
+    head_width = wg_ref.shape[1]
+    depth = w_ref.shape[0]
+    pending = []
+
+    def when(cond, act):
+        if cond is True:
+            act()
+        else:
+            pl.when(cond)(act)
+
+    def both(*conds):
+        out = True
+        for cond in conds:
+            if cond is not True:
+                out = cond if out is True else jnp.logical_and(out, cond)
+        return out
+
+    def count(zp):
+        return rows if zp < 2 else tail
+
+    def move(zp, yp, xp, half, way, device):
+        row = pl.multiple_of(2 * rows * zp + (rows * yp if zp < 2 else 0), 16)
+        column = pl.multiple_of(width * xp + half_width * half, 128)
+        part = x_ref.at[pl.ds(row, count(zp)), pl.ds(column, half_width)]
+        at = ((zp * 2 + yp) * 2 + xp) * 2 + half
+        return pltpu.make_async_remote_copy(
+            src_ref=part,
+            dst_ref=part,
+            send_sem=tsend.at[at, way],
+            recv_sem=trecv.at[at],
+            device_id=device,
+            device_id_type=MESH,
+        )
+
+    def send(cond, copy):
+        when(cond, copy.start)
+        pending.append((cond, copy))
+
+    def core_has(zp):
+        return True if zp < 2 else c == 0
+
+    def row_has(zp, near):
+        if zp < 2:
+            return True
+        return y == 0 if near else y == 1
+
+    greet(seq, s, t, 1)
+
+    for zp in range(3):
+        row = pl.multiple_of(2 * rows * zp + (rows * y if zp < 2 else 0), 16)
+        own = pltpu.make_async_copy(
+            tok_ref.at[pl.ds(0, count(zp)), :],
+            x_ref.at[pl.ds(row, count(zp)), pl.ds(pl.multiple_of(width * t, 128), width)],
+            own_sem,
+        )
+        cond = both(core_has(zp), row_has(zp, True), z == zp)
+        when(cond, own.start)
+        when(cond, own.wait)
+
+    def spread(zp, half, base):
+        send(both(base, z >= zp, z < 3), move(zp, y, t, half, 0, (lax.rem(s + 4, seq), t)))
+        send(both(base, z <= zp, z > 0), move(zp, y, t, half, 1, (lax.rem(s + seq - 4, seq), t)))
+        first, second = (2, 3) if half == 0 else (3, 2)
+        for way in (first, second):
+            device = (y_side, t) if way == 2 else (s, 1 - t)
+            send(base, move(zp, y, t, half, way, device))
+
+    for zp in range(3):
+        for half in range(2):
+            spread(zp, half, both(core_has(zp), row_has(zp, True), z == zp))
+
+    def slab(source, head_at, send_sem, recv_sem, device):
+        return pltpu.make_async_remote_copy(
+            src_ref=w_ref.at[:, pl.ds(pl.multiple_of(head_at * head_width, 128), head_width)],
+            dst_ref=wg_ref.at[pl.ds(pl.multiple_of(source * depth, 128), depth), :],
+            send_sem=send_sem,
+            recv_sem=recv_sem,
+            device_id=device,
+            device_id_type=MESH,
+        )
+
+    me = s // 2
+    mine = pltpu.make_async_copy(
+        w_ref.at[:, pl.ds(pl.multiple_of(me * head_width, 128), head_width)],
+        wg_ref.at[pl.ds(pl.multiple_of(s * depth, 128), depth), :],
+        wown,
+    )
+    mine.start()
+
+    def pair_at(step):
+        return lax.rem(me + step, pairs)
+
+    for step in range(1, pairs):
+        to = pair_at(step)
+        slab(s, to, wsend.at[step], wrecv.at[step], (2 * to + c, t)).start()
+
+    def onward(source, step):
+        part = wg_ref.at[pl.ds(pl.multiple_of(source * depth, 128), depth), :]
+        return pltpu.make_async_remote_copy(
+            src_ref=part,
+            dst_ref=part,
+            send_sem=fsend.at[step],
+            recv_sem=frecv.at[step],
+            device_id=(core_side, t),
+            device_id_type=MESH,
+        )
+
+    for zp in (1, 0, 2):
+        for half in range(2):
+            base = both(core_has(zp), row_has(zp, True), z != zp)
+            when(base, move(zp, y, t, half, 0, (s, 1 - t)).wait_recv)
+            spread(zp, half, base)
+        near = both(core_has(zp), row_has(zp, True))
+        far = both(core_has(zp), row_has(zp, False))
+        when(far, move(zp, 1 - y, t, 0, 0, (s, 1 - t)).wait_recv)
+        send(far, move(zp, 1 - y, t, 0, 3, (s, 1 - t)))
+        when(near, move(zp, y, 1 - t, 1, 0, (s, 1 - t)).wait_recv)
+        send(near, move(zp, y, 1 - t, 1, 2, (y_side, t)))
+
+    mine.wait()
+    onward(s, 0).start()
+    for step in range(1, pairs):
+        source = 2 * lax.rem(me + pairs - step, pairs) + c
+        slab(source, 0, wsend.at[step], wrecv.at[step], (core_side, t)).wait_recv()
+        onward(source, step).start()
+
+    for zp in (1, 0, 2):
+        near = both(core_has(zp), row_has(zp, True))
+        far = both(core_has(zp), row_has(zp, False))
+        when(near, move(zp, y, 1 - t, 0, 0, (s, 1 - t)).wait_recv)
+        when(far, move(zp, 1 - y, 1 - t, 0, 0, (s, 1 - t)).wait_recv)
+        when(far, move(zp, 1 - y, t, 1, 0, (s, 1 - t)).wait_recv)
+        when(far, move(zp, 1 - y, 1 - t, 1, 0, (s, 1 - t)).wait_recv)
+    for step in range(pairs):
+        source = 2 * lax.rem(me + pairs - step, pairs) + c
+        onward(source, step).wait_send()
+        onward(source + 1 - 2 * c, step).wait_recv()
+        if step:
+            to = pair_at(step)
+            slab(s, to, wsend.at[step], wrecv.at[step], (2 * to + c, t)).wait_send()
+    for cond, copy in pending:
+        when(cond, copy.wait_send)
+
+
+def gather_inputs(tokens, weights, seq, tail):
+    rows, width = tokens.shape
+    head_width = weights.shape[1] // (seq // 2)
+    dma = pltpu.SemaphoreType.DMA
+    return pl.pallas_call(
+        lambda *refs: gather_kernel(seq, tail, *refs),
+        out_shape=(
+            jax.ShapeDtypeStruct((4 * rows + tail, 2 * width), tokens.dtype),
+            jax.ShapeDtypeStruct((weights.shape[0] * seq, head_width), weights.dtype),
+        ),
+        in_specs=[pl.BlockSpec(memory_space=pl.ANY)] * 2,
+        out_specs=[pl.BlockSpec(memory_space=pl.ANY)] * 2,
+        scratch_shapes=[
+            dma,
+            dma((24, 4)),
+            dma((24,)),
+            dma,
+            dma((seq // 2,)),
+            dma((seq // 2,)),
+            dma((seq // 2,)),
+            dma((seq // 2,)),
+        ],
+        compiler_params=pltpu.CompilerParams(collective_id=0, has_side_effects=True),
+        name="gather_inputs",
+    )(tokens, weights)
+
+
+def owners_kernel(seq, rows, tail, att_ref, out_ref, own_sem, msend, mrecv, hsend, hrecv):
+    s = lax.axis_index("seq")
+    t = lax.axis_index("tp")
+    c = s % 2
+    head = s // 2
+    pairs = seq // 2
+    size = att_ref.shape[1]
+    greet(seq, s, t, 0)
+
+    def place(head_at):
+        return pl.ds(pl.multiple_of(head_at * size, 128), size)
+
+    def main(slot, number, from_head, device):
+        return pltpu.make_async_remote_copy(
+            src_ref=att_ref.at[pl.ds(rows * slot, number), :],
+            dst_ref=out_ref.at[pl.ds(0, number), place(from_head)],
+            send_sem=msend.at[slot],
+            recv_sem=mrecv.at[from_head],
+            device_id=device,
+            device_id_type=MESH,
+        )
+
+    def halo(slot, from_head, device):
+        return pltpu.make_async_remote_copy(
+            src_ref=att_ref.at[pl.ds(rows * slot, HALO), :],
+            dst_ref=out_ref.at[pl.ds(rows, HALO), place(from_head)],
+            send_sem=hsend.at[slot],
+            recv_sem=hrecv.at[from_head],
+            device_id=device,
+            device_id_type=MESH,
+        )
+
+    def each_slot(remote_act, local_act, halo_act):
+        for slot in range(5):
+            number = rows if slot < 4 else tail
+            owner = 2 * slot + c
+            there = True if slot < 4 else c == 0
+            away = jnp.logical_and(owner != s, there)
+            here = jnp.logical_and(owner == s, there)
+            copy = main(slot, number, head, (owner, t))
+            pl.when(away)(lambda: remote_act(copy))
+            own = pltpu.make_async_copy(
+                att_ref.at[pl.ds(rows * slot, number), :],
+                out_ref.at[pl.ds(0, number), place(head)],
+                own_sem,
+            )
+            pl.when(here)(lambda: local_act(own))
+            edge = halo(slot, head, (lax.rem(owner + seq - 1, seq), t))
+            pl.when(jnp.logical_and(owner >= 1, there))(lambda: halo_act(edge))
+
+    each_slot(lambda copy: copy.start(), lambda own: own.start(), lambda edge: edge.start())
+
+    for from_head in range(pairs):
+        sender = 2 * from_head + c
+        for number, cond in ((rows, s < 8), (tail, s == 8)):
+            arrived = main(0, number, from_head, (lax.rem(s + 1, seq), t))
+            pl.when(jnp.logical_and(cond, sender != s))(arrived.wait_recv)
+        pl.when(s < 8)(halo(0, from_head, (lax.rem(s + 1, seq), t)).wait_recv)
+
+    each_slot(lambda copy: copy.wait_send(), lambda own: own.wait(), lambda edge: edge.wait_send())
+
+
+def to_owners(attended, seq, rows, tail):
+    dma = pltpu.SemaphoreType.DMA
+    pairs = seq // 2
+    return pl.pallas_call(
+        lambda *refs: owners_kernel(seq, rows, tail, *refs),
+        out_shape=jax.ShapeDtypeStruct((rows + HALO, pairs * attended.shape[1]), attended.dtype),
+        in_specs=[pl.BlockSpec(memory_space=pl.ANY)],
+        out_specs=pl.BlockSpec(memory_space=pl.ANY),
+        scratch_shapes=[dma, dma((5,)), dma((pairs,)), dma((5,)), dma((pairs,))],
+        compiler_params=pltpu.CompilerParams(collective_id=1, has_side_effects=True),
+        name="to_owners",
+    )(attended)
+
+
+def head_body(tokens, ln_gain, ln_bias, w_qkv, w_out, layer_scale, grids, offsets):
+    rows, width = tokens.shape
+    seq = lax.axis_size("seq")
+    row_count = rows * seq
+    s = lax.axis_index("seq")
+    tp = lax.axis_index("tp")
+    core = s % 2
+    tail = -(-(PAIR_ROWS - 8 * rows) // 16) * 16
+    token_halo = from_behind(tokens[:HALO], "seq", -1)
+    out_weights = lax.all_gather(w_out, "seq", axis=2, tiled=True)
+    gathered, weights = gather_inputs(tokens, w_qkv.reshape(w_qkv.shape[0], -1), seq, tail)
+    widened = gathered.astype(jnp.float32)
+    average = jnp.mean(widened, axis=-1, keepdims=True)
+    spread_sq = jnp.mean(jnp.square(widened - average), axis=-1, keepdims=True)
+    normed = ((widened - average) * lax.rsqrt(spread_sq + 1e-06) * ln_gain + ln_bias).astype(
+        jnp.bfloat16
+    )
+    size = weights.shape[1] // 3
+    qkv_sums = jnp.dot(normed, weights, preferred_element_type=jnp.float32).reshape(-1, 3, size)
+
+    slot_rows = jnp.arange(gathered.shape[0], dtype=jnp.int32)
+    base_rows = (slot_rows // rows) * (2 * rows) + slot_rows % rows
+    row_ids = base_rows + core * rows
+    other_ids = base_rows + (1 - core) * rows
+    segment, inside, is_patch, grid_row, grid_col, grid_side = layout_rows(
+        row_ids, offsets, grids, row_count
+    )
+    turned = rotate(qkv_sums[:, :2], is_patch, grid_row, grid_col, grid_side)
+    queries = turned[:, 0].astype(jnp.bfloat16)
+    keys_values = jnp.concatenate([turned[:, 1], qkv_sums[:, 2]], axis=-1).astype(jnp.bfloat16)
+    keys_values = jnp.where(inside[:, None], keys_values, jnp.zeros_like(keys_values))
+    others = lax.ppermute(keys_values, "seq", [(i, i ^ 1) for i in range(seq)])
+    all_kv = jnp.concatenate([keys_values, others], axis=0)
+    other_layout = layout_rows(other_ids, offsets, grids, row_count)
+    key_segment = jnp.concatenate([segment, other_layout[0]])
+    key_inside = jnp.concatenate([inside, other_layout[1]])
+    allowed = inside[:, None] & key_inside[None, :] & (segment[:, None] == key_segment[None, :])
+    logits = jnp.dot(
+        queries, all_kv[:, :size].T, preferred_element_type=jnp.float32
+    ) * (1.0 / math.sqrt(size))
+    masked = jnp.where(allowed, logits, -1e30)
+    row_max = jnp.max(masked, axis=1, keepdims=True)
+    terms = jnp.where(allowed, jnp.exp(masked - row_max), 0.0)
+    total = jnp.where(inside[:, None], jnp.sum(terms, axis=1, keepdims=True), 1.0)
+    soft = (terms / total).astype(jnp.bfloat16)
+    attended = jnp.dot(soft, all_kv[:, size:], preferred_element_type=jnp.float32)
+    attended = jnp.where(inside[:, None], attended, 0.0).astype(jnp.bfloat16)
+
+    mine = to_owners(attended, seq, rows, tail)
+    projected = jnp.dot(
+        mine, out_weights.reshape(mine.shape[1], -1), preferred_element_type=jnp.float32
+    ).astype(jnp.bfloat16)
+    kept = lax.dynamic_slice_in_dim(projected, tp * width, width, 1)
+    given = lax.dynamic_slice_in_dim(projected, (1 - tp) * width, width, 1)
+    taken = lax.ppermute(given, "tp", [(0, 1), (1, 0)])
+    head_total = kept.astype(jnp.float32) + taken.astype(jnp.float32)
+    extended_tokens = jnp.concatenate([tokens, token_halo], axis=0).astype(jnp.float32)
+    extended = (extended_tokens + layer_scale * head_total).astype(jnp.bfloat16)
+
+    local_ids = jnp.arange(rows, dtype=jnp.int32)
+    _, _, is_patch, grid_row, grid_col, grid_side = layout_rows(
+        s * rows + local_ids, offsets, grids, row_count
+    )
+    is_corner = is_patch & (grid_row % 2 == 0) & (grid_col % 2 == 0)
+    corner_index = jnp.stack(
+        [local_ids, local_ids + 1, local_ids + grid_side, local_ids + grid_side + 1], axis=1
+    )
+    corner_index = jnp.clip(corner_index, 0, extended.shape[0] - 1)
+    merged = jnp.take(extended, corner_index, axis=0)
+    return jnp.where(is_corner[:, None, None], merged, jnp.zeros_like(merged))
+
+
 def solution(mesh):
     placed = (
         P("seq", "tp"),
@@ -201,6 +551,11 @@
         P(),
         P(),
     )
+    small = mesh.shape["seq"] == 16 and mesh.shape["tp"] == 2
     return jax.shard_map(
-        body, mesh=mesh, in_specs=placed, out_specs=P("seq", None, "tp"), check_vma=False
-    )
+        head_body if small else window_body,
+        mesh=mesh,
+        in_specs=placed,
+        out_specs=P("seq", None, "tp"),
+        check_vma=False,
+    )

time: 798 us -> 341 us (0.43)
  waiting for transfers between devices: 482 us -> 21.9 us
  Pallas kernels: 0 us -> 222 us
  starting transfers between devices: 96.7 us -> 5.65 us
  local copies, waits for them, and re-layouts: 99.3 us -> 27.2 us
  matrix products: 74.1 us -> 21.9 us
    ppermute x15 -> x1, waiting for transfers between devices: 264 us -> 0.01 us  [from_behind(): return lax.ppermute(shard, axis, pairs)]
    pallas_call x0 -> x2, Pallas kernels: none -> 222 us  [the longest x1 150 us: gather_inputs(): pl.pallas_call(lambda *refs: gather_kernel(seq, tail, *refs), out_shape=(...]
    all_gather x3 -> x1, waiting for transfers between devices: 167 us -> 0.02 us  [head_body(): out_weights = lax.all_gather(w_out, 'seq', axis=2, tiled=True)]
    ppermute x15 -> x1, starting transfers between devices: 96.6 us -> 1.92 us  [from_behind(): return lax.ppermute(shard, axis, pairs)]
    reduce_scatter x1 -> x0, waiting for transfers between devices: 50.8 us -> none  [body(): lax.psum_scatter(projected.astype(jnp.bfloat16), 'tp', scatter_dimension=...]
    dot_general x31 -> x4, matrix products: 61.9 us -> 21.9 us  [the longest x1 6.73 us: head_body(): jnp.dot(normed, weights, preferred_element_type=jnp.float32)]
    unnamed x31 -> x19, local copies, waits for them, and re-layouts: 44.1 us -> 6.13 us
    squeeze x31 -> x2, local copies, waits for them, and re-layouts: 39.2 us -> 1.22 us  [the longest x1 1.19 us: head_body(): qkv_sums[:, 2]]
  transfers between devices with their start and end apart: 19 -> 4, of which waited for: 14 -> 1; matrix products, arithmetic and copies ran while one was open for 20% -> 15% of each run, Pallas kernels for 0% -> 65%
where the time goes in v1:
time: 341 us; the launch traced here: 339 us
  Pallas kernels  222 us (65%)
  local copies, waits for them, and re-layouts  27.2 us (8%)
  other arithmetic  26.9 us (8%)
  waiting for transfers between devices  21.9 us (6%)
  matrix products  21.9 us (6%)
  between operations  13.7 us (4%)
  starting transfers between devices  5.65 us (2%)
    pallas_call x1, Pallas kernels, gather_inputs(): pl.pallas_call(lambda *refs: gather_kernel(seq, tail, *refs), out_shape=(...  150 us
    pallas_call x1, Pallas kernels, to_owners(): pl.pallas_call(lambda *refs: owners_kernel(seq, rows, tail, *refs), out_s...  72.2 us
    ppermute x1, waiting for transfers between devices, head_body(): taken = lax.ppermute(given, 'tp', [(0, 1), (1, 0)])  21.1 us
    gather x2, local copies, waits for them, and re-layouts, head_body(): merged = jnp.take(extended, corner_index, axis=0)  13.2 us
  transfers between devices with their start and end apart: 4, of which 1 were waited for; matrix products, arithmetic and copies ran while one was open for 15% of the time, Pallas kernels for 65%

profile of v1, /device:TPU:5, one launch (start us, length us, event | category | flops | bytes accessed | tf_op | source)
XLA Modules:
  0.0 339.4 jit_solution(8299263391559139045)
XLA Ops:
  7.3 2.2 copy.37
  9.4 1.7 copy.38.refs_1_
  11.2 150.0 %gather_inputs.1 = (bf16[1168,4096]{1,0:T(8,128)(2,1)}, bf16[4096,384]{1,0:T(8,128)(2,1)}) custom-call(bf16[256,2048]{1,0:T(8,128)(2,1)} %refs_0_.1, bf16[256,3072]{1,0:T(8,128)(2,1)} %copy.38.refs_1_), custom_call_target="tpu_custom_call" | custom-call | tf_op jit(solution)/shard_map/gather_inputs/pallas_call | solution.py:372
  161.6 5.2 %convert_reduce_fusion = f32[1168]{0:T(1024)S(1)} fusion(bf16[1168,4096]{1,0:T(8,128)(2,1)} %get-tuple-element.7), kind=kLoop, calls=%fused_computation.2 | loop fusion | flops 9567088 | bytes 9572928 | tf_op jit(solution)/shard_map/reduce_sum | solution.py:483
  166.8 1.2 copy-done
  168.0 2.6 fusion.2
  170.9 1.2 fusion.20
  172.1 6.7 %fusion.7 = f32[1168,384]{0,1:T(8,128)S(1)} fusion(bf16[4096,384]{1,0:T(8,128)(2,1)} %get-tuple-element.8, bf16[1168,4096]{1,0:T(8,128)(2,1)S(1)} %copy-done, f32[4096]{0:T(1024)S(1)} %copy-done.7, f32[4096]{0:T(1024)S(1)} %copy-done.8, f32[1168]{0:T(1024)S(1)} %add_rsqrt_fusion, f32[1168]{0:T(1024)S(1)} %broadcast_multiply_fusion), kind=kOutput, calls=%fused_computation.14 | convolution fusion | flops 3702915072 | bytes 14550144 | tf_op jit(solution)/shard_map/dot_general | solution.py:489
  178.9 1.3 copy-done.3
  182.1 3.4 %collective-permute-start.1 = (bf16[1168,256]{1,0:T(8,128)(2,1)S(1)}, bf16[1168,256]{1,0:T(8,128)(2,1)}, u32[]{:S(2)}, u32[]{:S(2)}) collective-permute-start(bf16[1168,256]{1,0:T(8,128)(2,1)S(1)} %copy.42), channel_id=1, source_target_pairs={{0,2},{2,0},{4,6},{6,4},{8,10},{10,8},{12,14},{14,12},{16,18},{18,... | collective-permute-start | bytes 1794056 | tf_op jit(solution)/shard_map/ppermute | solution.py:502
  186.2 1.9 collective-permute-start
  188.4 1.3 copy.43
  189.7 3.6 %fusion.55 = (f32[1168]{0:T(1024)S(1)}, f32[1168,2336]{1,0:T(8,128)S(1)}) fusion(bf16[1168,256]{0,1:T(8,128)(2,1)S(1)} %maximum_select_fusion, bf16[1168,256]{0,1:T(8,128)(2,1)S(1)} %copy.43, bf16[1168,2,128]{0,2,1:T(8,128)(2,1)S(1)} %maximum_convert_fusion, s32[2336]{0:T(1024)S(1)} %pad_add_fusion, s32[1168]{0:T(1024)S(1)} %get-tuple-element.13, ...), kind=kOutput, calls=%fused_computation.130 | convolution fusion | flops 716048256 | bytes 12582464 | tf_op jit(solution)/shard_map/dot_general | solution.py:508
  193.3 3.9 %fusion.9 = f32[1168]{0:T(1024)S(1)} fusion(f32[1168,2336]{1,0:T(8,128)S(1)} %get-tuple-element.38, f32[1168]{0:T(1024)S(1)} %get-tuple-element.37, s32[2336]{0:T(1024)S(1)} %pad_add_fusion, s32[1168]{0:T(1024)S(1)} %get-tuple-element.13, pred[2336]{0:T(1024)(128)(4,1)S(1)} %pad_add_fusion.1, pred[1168]{0:T(1024)(128)(4,1)S(1)} %get-tuple-element.16), kind=kLoop, calls=%fused_computation.15 | loop fusion | flops 16369520 | bytes 10940656 | tf_op jit(solution)/shard_map/reduce_sum | solution.py:514
  197.2 5.2 %fusion.12.refs_0_ = bf16[1168,128]{1,0:T(8,128)(2,1)} fusion(f32[1168,2336]{1,0:T(8,128)S(1)} %get-tuple-element.38, f32[1168]{0:T(1024)S(1)} %broadcast_select_fusion, f32[1168]{0:T(1024)S(1)} %get-tuple-element.37, s32[2336]{0:T(1024)S(1)} %pad_add_fusion, s32[1168]{0:T(1024)S(1)} %get-tuple-element.13, pred[2336]{0:T(1024)(128)(4,1)S(1)} %pad_add_fusion.1, ...), kind=kOutput, calls=%fused_computation.21 | convolution fusion | flops 719076864 | bytes 12435696 | tf_op jit(solution)/shard_map/dot_general | solution.py:516
  202.5 72.2 %to_owners.1 = bf16[304,1024]{1,0:T(8,128)(2,1)} custom-call(bf16[1168,128]{1,0:T(8,128)(2,1)} %fusion.12.refs_0_), custom_call_target="tpu_custom_call" | custom-call | tf_op jit(solution)/shard_map/to_owners/pallas_call | solution.py:460
  274.7 6.3 %convolution_convert_fusion = bf16[304,4096]{1,0:T(8,128)(2,1)S(1)} fusion(bf16[304,1024]{1,0:T(8,128)(2,1)} %to_owners.1, bf16[1024,4096]{1,0:T(8,128)(2,1)} %bitcast.28), kind=kOutput, calls=%fused_computation.17 | convolution fusion | flops 2551382016 | bytes 11501568 | tf_op jit(solution)/shard_map/dot_general | solution.py:520
  281.0 1.4 copy-done.2
  283.5 1.3 select_reduce_fusion.3
  290.1 21.1 %collective-permute-done.2 = bf16[304,2048]{1,0:T(8,128)(2,1)S(1)} collective-permute-done((bf16[304,2048]{1,0:T(8,128)(2,1)S(1)}, bf16[304,2048]{1,0:T(8,128)(2,1)S(1)}, u32[]{:S(2)}, u32[]{:S(2)}) %collective-permute-start.2) | collective-permute-done | bytes 1245216 | tf_op jit(solution)/shard_map/ppermute | solution.py:525
  311.2 2.0 add_convert_fusion
  313.3 6.0 %gather_fusion = bf16[1024,2048]{1,0:T(8,128)(2,1)} fusion(bf16[304,2048]{1,0:T(8,128)(2,1)S(1)} %add_convert_fusion, s32[1024]{0:T(1024)S(1)} %broadcast_clamp_fusion), kind=kCustom, calls=%fused_computation | custom fusion | bytes 8392704 | tf_op jit(solution)/shard_map/jit(_take)/gather | solution.py:539
  319.2 7.2 %reshape.456 = bf16[256,4,2048]{2,1,0:T(4,128)(2,1)} reshape(bf16[1024,2048]{1,0:T(8,128)(2,1)} %gather_fusion) | data formatting | bytes 8388608 | tf_op jit(solution)/shard_map/jit(_take)/gather | solution.py:539
  326.4 6.1 %select_select_fusion = bf16[256,4,2048]{2,1,0:T(4,128)(2,1)} fusion(bf16[256,4,2048]{2,1,0:T(4,128)(2,1)} %reshape.456, pred[256]{0:T(512)(128)(4,1)S(1)} %compare_and_fusion.5, pred[256,4]{1,0:T(8,128)(4,1)S(1)} %copy-done.4), kind=kLoop, calls=%fused_computation.18 | loop fusion | flops 4194304 | bytes 8389888 | tf_op jit(solution)/shard_map/jit(_where)/select_n | solution.py:540
  (57 shorter events, 10.6 us)
Async XLA Ops:
  6.5 268.1 %all-gather.2.cloned.1.call-start = ((), (), s32[]{:S(2)}) async-start(), calls=%async_computation | async-start | bytes 8912896 | tf_op jit(solution)/shard_map/all_gather | solution.py:480
  9.4 151.8 %copy-start.5 = (s32[3]{0:T(128)S(1)}, s32[3]{0:T(128)}, u32[]{:S(2)}) copy-start(s32[3]{0:T(128)} %param.15) | copy-start | bytes 40
  9.4 152.0 %copy-start.6 = (s32[2]{0:T(128)S(1)}, s32[2]{0:T(128)}, u32[]{:S(2)}) copy-start(s32[2]{0:T(128)} %param.14) | copy-start | bytes 28
  161.6 6.4 %copy-start = (bf16[1168,4096]{1,0:T(8,128)(2,1)S(1)}, bf16[1168,4096]{1,0:T(8,128)(2,1)}, u32[]{:S(2)}) copy-start(bf16[1168,4096]{1,0:T(8,128)(2,1)} %get-tuple-element.7) | copy-start | bytes 28704772
  168.0 4.1 %copy-start.7 = (f32[4096]{0:T(1024)S(1)}, f32[4096]{0:T(1024)}, u32[]{:S(2)}) copy-start(f32[4096]{0:T(1024)} %param.10) | copy-start | bytes 49156
  168.0 4.1 %copy-start.8 = (f32[4096]{0:T(1024)S(1)}, f32[4096]{0:T(1024)}, u32[]{:S(2)}) copy-start(f32[4096]{0:T(1024)} %param.9) | copy-start | bytes 49156
  178.8 1.3 copy-start.3
  180.5 5.1 %copy-start.1 = (bf16[256,2048]{1,0:T(8,128)(2,1)S(1)}, bf16[256,2048]{1,0:T(8,128)(2,1)}, u32[]{:S(2)}) copy-start(bf16[256,2048]{1,0:T(8,128)(2,1)} %refs_0_.1) | copy-start | bytes 3145732
  182.1 6.3 %collective-permute-start.1 = (bf16[1168,256]{1,0:T(8,128)(2,1)S(1)}, bf16[1168,256]{1,0:T(8,128)(2,1)}, u32[]{:S(2)}, u32[]{:S(2)}) collective-permute-start(bf16[1168,256]{1,0:T(8,128)(2,1)S(1)} %copy.42), channel_id=1, source_target_pairs={{0,2},{2,0},{4,6},{6,4},{8,10},{10,8},{12,14},{14,12},{16,18},{18,... | collective-permute-start | bytes 1794056 | tf_op jit(solution)/shard_map/ppermute | solution.py:502
  186.2 103.9 %collective-permute-start = (bf16[48,2048]{1,0:T(8,128)(2,1)}, bf16[48,2048]{1,0:T(8,128)(2,1)}, u32[]{:S(2)}, u32[]{:S(2)}) collective-permute-start(bf16[48,2048]{1,0:T(8,128)(2,1)} %slice.53), channel_id=1, source_target_pairs={{2,0},{4,2},{6,4},{8,6},{10,8},{12,10},{14,12},{16,14},{18,16},{20... | collective-permute-start | bytes 589832 | tf_op jit(solution)/shard_map/ppermute | solution.py:17
  281.0 1.5 copy-start.2
  282.5 28.7 %collective-permute-start.2 = (bf16[304,2048]{1,0:T(8,128)(2,1)S(1)}, bf16[304,2048]{1,0:T(8,128)(2,1)S(1)}, u32[]{:S(2)}, u32[]{:S(2)}) collective-permute-start(bf16[304,2048]{1,0:T(8,128)(2,1)S(1)} %constant_dynamic-slice_fusion), channel_id=1, source_target_pairs={{0,1},{1,0},{2,3},{3,2},{4,5},{5,4},{6,7},{7,6},{8,9},{9,8},{10,11... | collective-permute-start | bytes 3735560 | tf_op jit(solution)/shard_map/ppermute | solution.py:525
  319.2 7.2 %copy-start.4 = (pred[256,4]{1,0:T(8,128)(4,1)S(1)}, pred[256,4]{1,0:T(8,128)(4,1)}, u32[]{:S(2)}) copy-start(pred[256,4]{1,0:T(8,128)(4,1)} %copy.36) | copy-start | bytes 3076
Sparse Core Ops, SparseCore 0:
  9.5 126.6 all-gather.1

commit v2 on v1

--- a/solution.py
+++ b/solution.py
@@ -196,22 +196,39 @@
 MESH = pl.DeviceIdType.MESH
 
 
-def greet(seq, s, t, across):
+def greet(seq, s, t):
     barrier = pltpu.get_barrier_semaphore()
-
-    @pl.loop(1, seq)
+    own = 2 * s + t
+
+    @pl.loop(1, 2 * seq)
     def _(i):
+        other = lax.rem(own + i, 2 * seq)
         pl.semaphore_signal(
-            barrier, inc=1, device_id=(lax.rem(s + i, seq), t), device_id_type=MESH
-        )
-
-    if across:
-        pl.semaphore_signal(barrier, inc=1, device_id=(s, 1 - t), device_id_type=MESH)
-    pl.semaphore_wait(barrier, seq - 1 + across)
+            barrier, inc=1, device_id=(other // 2, lax.rem(other, 2)), device_id_type=MESH
+        )
+
+    pl.semaphore_wait(barrier, 2 * seq - 1)
 
 
 def gather_kernel(
-    seq, tail, tok_ref, w_ref, x_ref, wg_ref, own_sem, tsend, trecv, wown, wsend, wrecv, fsend, frecv
+    seq,
+    tail,
+    tok_ref,
+    w_ref,
+    o_ref,
+    x_ref,
+    wg_ref,
+    og_ref,
+    own_sem,
+    tsend,
+    trecv,
+    wown,
+    wsend,
+    wrecv,
+    fsend,
+    frecv,
+    osend,
+    orecv,
 ):
     s = lax.axis_index("seq")
     t = lax.axis_index("tp")
@@ -267,7 +284,7 @@
             return True
         return y == 0 if near else y == 1
 
-    greet(seq, s, t, 1)
+    greet(seq, s, t)
 
     for zp in range(3):
         row = pl.multiple_of(2 * rows * zp + (rows * y if zp < 2 else 0), 16)
@@ -313,9 +330,41 @@
     def pair_at(step):
         return lax.rem(me + step, pairs)
 
-    for step in range(1, pairs):
-        to = pair_at(step)
-        slab(s, to, wsend.at[step], wrecv.at[step], (2 * to + c, t)).start()
+    def send_slabs(upward):
+        for step in range(1, pairs):
+            to = pair_at(step)
+            slab_copy = slab(s, to, wsend.at[step], wrecv.at[step], (2 * to + c, t))
+            pl.when((to // 2 > z) if upward else (to // 2 <= z))(slab_copy.start)
+
+    send_slabs(False)
+
+    out_rows, out_columns = o_ref.shape
+    piece = out_columns // 2
+    goes = [(2 * lax.rem(s, pairs) + u, s // pairs) for u in range(2)]
+    comes = pairs * t + s // 2
+
+    def column_block(u, into, device):
+        return pltpu.make_async_remote_copy(
+            src_ref=o_ref.at[:, pl.ds(piece * u, piece)],
+            dst_ref=og_ref.at[pl.ds(pl.multiple_of(out_rows * into, 128), out_rows), :],
+            send_sem=osend.at[u],
+            recv_sem=orecv.at[into],
+            device_id=device,
+            device_id_type=MESH,
+        )
+
+    def column_blocks(remote_act, local_act):
+        for u in range(2):
+            to_s, to_t = goes[u]
+            stays = jnp.logical_and(to_s == s, to_t == t)
+            copy = column_block(u, t, (to_s, to_t))
+            local = pltpu.make_async_copy(
+                o_ref.at[:, pl.ds(piece * u, piece)],
+                og_ref.at[pl.ds(pl.multiple_of(out_rows * t, 128), out_rows), :],
+                osend.at[u],
+            )
+            pl.when(jnp.logical_not(stays))(lambda: remote_act(copy))
+            pl.when(stays)(lambda: local_act(local))
 
     def onward(source, step):
         part = wg_ref.at[pl.ds(pl.multiple_of(source * depth, 128), depth), :]
@@ -340,6 +389,8 @@
         when(near, move(zp, y, 1 - t, 1, 0, (s, 1 - t)).wait_recv)
         send(near, move(zp, y, 1 - t, 1, 2, (y_side, t)))
 
+    send_slabs(True)
+    column_blocks(lambda copy: copy.start(), lambda local: local.start())
     mine.wait()
     onward(s, 0).start()
     for step in range(1, pairs):
@@ -361,11 +412,15 @@
         if step:
             to = pair_at(step)
             slab(s, to, wsend.at[step], wrecv.at[step], (2 * to + c, t)).wait_send()
+    column_blocks(lambda copy: copy.wait_send(), lambda local: local.wait())
+    for into in range(2):
+        remote = jnp.logical_or(comes != s, into != t)
+        pl.when(remote)(column_block(0, into, (core_side, t)).wait_recv)
     for cond, copy in pending:
         when(cond, copy.wait_send)
 
 
-def gather_inputs(tokens, weights, seq, tail):
+def gather_inputs(tokens, weights, out_weights, seq, tail):
     rows, width = tokens.shape
     head_width = weights.shape[1] // (seq // 2)
     dma = pltpu.SemaphoreType.DMA
@@ -374,9 +429,12 @@
         out_shape=(
             jax.ShapeDtypeStruct((4 * rows + tail, 2 * width), tokens.dtype),
             jax.ShapeDtypeStruct((weights.shape[0] * seq, head_width), weights.dtype),
+            jax.ShapeDtypeStruct(
+                (2 * out_weights.shape[0], out_weights.shape[1] // 2), weights.dtype
+            ),
         ),
-        in_specs=[pl.BlockSpec(memory_space=pl.ANY)] * 2,
-        out_specs=[pl.BlockSpec(memory_space=pl.ANY)] * 2,
+        in_specs=[pl.BlockSpec(memory_space=pl.ANY)] * 3,
+        out_specs=[pl.BlockSpec(memory_space=pl.ANY)] * 3,
         scratch_shapes=[
             dma,
             dma((24, 4)),
@@ -386,39 +444,41 @@
             dma((seq // 2,)),
             dma((seq // 2,)),
             dma((seq // 2,)),
+            dma((2,)),
+            dma((2,)),
         ],
         compiler_params=pltpu.CompilerParams(collective_id=0, has_side_effects=True),
         name="gather_inputs",
-    )(tokens, weights)
+    )(tokens, weights, out_weights)
 
 
 def owners_kernel(seq, rows, tail, att_ref, out_ref, own_sem, msend, mrecv, hsend, hrecv):
     s = lax.axis_index("seq")
     t = lax.axis_index("tp")
     c = s % 2
-    head = s // 2
     pairs = seq // 2
+    head = pairs * t + s // 2
     size = att_ref.shape[1]
-    greet(seq, s, t, 0)
+    greet(seq, s, t)
 
     def place(head_at):
         return pl.ds(pl.multiple_of(head_at * size, 128), size)
 
-    def main(slot, number, from_head, device):
+    def main(slot, number, side, from_head, device):
         return pltpu.make_async_remote_copy(
             src_ref=att_ref.at[pl.ds(rows * slot, number), :],
             dst_ref=out_ref.at[pl.ds(0, number), place(from_head)],
-            send_sem=msend.at[slot],
+            send_sem=msend.at[slot, side],
             recv_sem=mrecv.at[from_head],
             device_id=device,
             device_id_type=MESH,
         )
 
-    def halo(slot, from_head, device):
+    def halo(slot, side, from_head, device):
         return pltpu.make_async_remote_copy(
             src_ref=att_ref.at[pl.ds(rows * slot, HALO), :],
             dst_ref=out_ref.at[pl.ds(rows, HALO), place(from_head)],
-            send_sem=hsend.at[slot],
+            send_sem=hsend.at[slot, side],
             recv_sem=hrecv.at[from_head],
             device_id=device,
             device_id_type=MESH,
@@ -429,43 +489,65 @@
             number = rows if slot < 4 else tail
             owner = 2 * slot + c
             there = True if slot < 4 else c == 0
-            away = jnp.logical_and(owner != s, there)
-            here = jnp.logical_and(owner == s, there)
-            copy = main(slot, number, head, (owner, t))
-            pl.when(away)(lambda: remote_act(copy))
             own = pltpu.make_async_copy(
                 att_ref.at[pl.ds(rows * slot, number), :],
                 out_ref.at[pl.ds(0, number), place(head)],
                 own_sem,
             )
-            pl.when(here)(lambda: local_act(own))
-            edge = halo(slot, head, (lax.rem(owner + seq - 1, seq), t))
-            pl.when(jnp.logical_and(owner >= 1, there))(lambda: halo_act(edge))
+            pl.when(jnp.logical_and(owner == s, there))(lambda: local_act(own))
+            for side in range(2):
+                to_t = t if side == 0 else 1 - t
+                copy = main(slot, number, side, head, (owner, to_t))
+                away = jnp.logical_and(owner != s, there) if side == 0 else there
+                pl.when(away)(lambda: remote_act(copy))
+                edge = halo(slot, side, head, (lax.rem(owner + seq - 1, seq), to_t))
+                pl.when(jnp.logical_and(owner >= 1, there))(lambda: halo_act(edge))
 
     each_slot(lambda copy: copy.start(), lambda own: own.start(), lambda edge: edge.start())
 
-    for from_head in range(pairs):
-        sender = 2 * from_head + c
+    for from_head in range(2 * pairs):
+        itself = jnp.logical_and(from_head % pairs == s // 2, from_head // pairs == t)
         for number, cond in ((rows, s < 8), (tail, s == 8)):
-            arrived = main(0, number, from_head, (lax.rem(s + 1, seq), t))
-            pl.when(jnp.logical_and(cond, sender != s))(arrived.wait_recv)
-        pl.when(s < 8)(halo(0, from_head, (lax.rem(s + 1, seq), t)).wait_recv)
+            arrived = main(0, number, 0, from_head, (s, 1 - t))
+            pl.when(jnp.logical_and(cond, jnp.logical_not(itself)))(arrived.wait_recv)
+        pl.when(s < 8)(halo(0, 0, from_head, (s, 1 - t)).wait_recv)
 
     each_slot(lambda copy: copy.wait_send(), lambda own: own.wait(), lambda edge: edge.wait_send())
 
 
 def to_owners(attended, seq, rows, tail):
     dma = pltpu.SemaphoreType.DMA
-    pairs = seq // 2
     return pl.pallas_call(
         lambda *refs: owners_kernel(seq, rows, tail, *refs),
-        out_shape=jax.ShapeDtypeStruct((rows + HALO, pairs * attended.shape[1]), attended.dtype),
+        out_shape=jax.ShapeDtypeStruct((rows + HALO, seq * attended.shape[1]), attended.dtype),
         in_specs=[pl.BlockSpec(memory_space=pl.ANY)],
         out_specs=pl.BlockSpec(memory_space=pl.ANY),
-        scratch_shapes=[dma, dma((5,)), dma((pairs,)), dma((5,)), dma((pairs,))],
+        scratch_shapes=[dma, dma((5, 2)), dma((seq,)), dma((5, 2)), dma((seq,))],
         compiler_params=pltpu.CompilerParams(collective_id=1, has_side_effects=True),
         name="to_owners",
     )(attended)
+
+
+def merge_kernel(pick_ref, rows_ref, out_ref):
+    count, four, width = out_ref.shape
+    picked = jnp.dot(pick_ref[...], rows_ref[...], preferred_element_type=jnp.float32)
+    out_ref[...] = picked.reshape(count, four, width).astype(out_ref.dtype)
+
+
+def merge_rows(pick, extended, count, step):
+    width = extended.shape[1]
+    return pl.pallas_call(
+        merge_kernel,
+        grid=(count // step,),
+        out_shape=jax.ShapeDtypeStruct((count, 4, width), extended.dtype),
+        in_specs=[
+            pl.BlockSpec((4 * step, pick.shape[1]), lambda i: (i, 0)),
+            pl.BlockSpec(extended.shape, lambda i: (0, 0)),
+        ],
+        out_specs=pl.BlockSpec((step, 4, width), lambda i: (i, 0, 0)),
+        compiler_params=pltpu.CompilerParams(vmem_limit_bytes=32 * 1024 * 1024),
+        name="merge_rows",
+    )(pick, extended)
 
 
 def head_body(tokens, ln_gain, ln_bias, w_qkv, w_out, layer_scale, grids, offsets):
@@ -477,8 +559,14 @@
     core = s % 2
     tail = -(-(PAIR_ROWS - 8 * rows) // 16) * 16
     token_halo = from_behind(tokens[:HALO], "seq", -1)
-    out_weights = lax.all_gather(w_out, "seq", axis=2, tiled=True)
-    gathered, weights = gather_inputs(tokens, w_qkv.reshape(w_qkv.shape[0], -1), seq, tail)
+    gathered, weights, columns = gather_inputs(
+        tokens,
+        w_qkv.reshape(w_qkv.shape[0], -1),
+        w_out.reshape(-1, w_out.shape[2]),
+        seq,
+        tail,
+    )
+    out_weights = lax.all_gather(columns, "seq", axis=1, tiled=True)
     widened = gathered.astype(jnp.float32)
     average = jnp.mean(widened, axis=-1, keepdims=True)
     spread_sq = jnp.mean(jnp.square(widened - average), axis=-1, keepdims=True)
@@ -517,15 +605,13 @@
     attended = jnp.where(inside[:, None], attended, 0.0).astype(jnp.bfloat16)
 
     mine = to_owners(attended, seq, rows, tail)
-    projected = jnp.dot(
-        mine, out_weights.reshape(mine.shape[1], -1), preferred_element_type=jnp.float32
-    ).astype(jnp.bfloat16)
-    kept = lax.dynamic_slice_in_dim(projected, tp * width, width, 1)
-    given = lax.dynamic_slice_in_dim(projected, (1 - tp) * width, width, 1)
-    taken = lax.ppermute(given, "tp", [(0, 1), (1, 0)])
-    head_total = kept.astype(jnp.float32) + taken.astype(jnp.float32)
+    head_total = jnp.dot(mine, out_weights, preferred_element_type=jnp.float32)
     extended_tokens = jnp.concatenate([tokens, token_halo], axis=0).astype(jnp.float32)
     extended = (extended_tokens + layer_scale * head_total).astype(jnp.bfloat16)
+    extended_ids = s * rows + jnp.arange(rows + HALO, dtype=jnp.int32)
+    extended = jnp.where(
+        (extended_ids < offsets[-1])[:, None], extended, jnp.zeros_like(extended)
+    )
 
     local_ids = jnp.arange(rows, dtype=jnp.int32)
     _, _, is_patch, grid_row, grid_col, grid_side = layout_rows(
@@ -535,9 +621,11 @@
     corner_index = jnp.stack(
         [local_ids, local_ids + 1, local_ids + grid_side, local_ids + grid_side + 1], axis=1
     )
-    corner_index = jnp.clip(corner_index, 0, extended.shape[0] - 1)
-    merged = jnp.take(extended, corner_index, axis=0)
-    return jnp.where(is_corner[:, None, None], merged, jnp.zeros_like(merged))
+    corner_index = jnp.where(is_corner[:, None], corner_index, -1).reshape(-1)
+    pick = (
+        corner_index[:, None] == jnp.arange(extended.shape[0], dtype=jnp.int32)[None, :]
+    ).astype(jnp.bfloat16)
+    return merge_rows(pick, extended, rows, 32)
 
 
 def solution(mesh):

time: 341 us -> 298 us (0.87)
  Pallas kernels: 222 us -> 201 us
  local copies, waits for them, and re-layouts: 27.2 us -> 9.42 us
  starting transfers between devices: 5.65 us -> 21.2 us
  other arithmetic: 26.9 us -> 15.1 us
  waiting for transfers between devices: 21.9 us -> 13.2 us
    ppermute x1 -> x0, waiting for transfers between devices: 21.1 us -> none  [head_body(): taken = lax.ppermute(given, 'tp', [(0, 1), (1, 0)])]
    ppermute x1, starting transfers between devices: 3.41 us -> 19.3 us  [head_body(): others = lax.ppermute(keys_values, 'seq', [(i, i ^ 1) for i in range(seq)])]
    pallas_call x1, Pallas kernels: 150 us -> 136 us  [gather_inputs(): pl.pallas_call(lambda *refs: gather_kernel(seq, tail, *refs), out_shape=(...]
    gather x2 -> x0, local copies, waits for them, and re-layouts: 13.2 us -> none  [head_body(): merged = jnp.take(extended, corner_index, axis=0)]
    all_gather x1, waiting for transfers between devices: 0.02 us -> 13.2 us  [head_body(): out_weights = lax.all_gather(columns, 'seq', axis=1, tiled=True)]
    pallas_call x1, Pallas kernels: 72.2 us -> 59.6 us  [to_owners(): pl.pallas_call(lambda *refs: owners_kernel(seq, rows, tail, *refs), out_s...]
    select_n x2 -> x1, other arithmetic: 6.76 us -> 0.01 us  [head_body(): corner_index = jnp.where(is_corner[:, None], corner_index, -1).reshape(-1)]
    pallas_call x0 -> x1, Pallas kernels: none -> 5.52 us  [merge_rows(): pl.pallas_call(merge_kernel, grid=(count // step,), out_shape=jax.ShapeDt...]
  transfers between devices with their start and end apart: 4 -> 3, of which waited for: 1 -> 1; matrix products, arithmetic and copies ran while one was open for 15% -> 12% of each run, Pallas kernels for 65% -> 20%
where the time goes in v2:
time: 298 us; the launch traced here: 297 us
  Pallas kernels  201 us (67%)
  matrix products  23.3 us (8%)
  starting transfers between devices  21.2 us (7%)
  other arithmetic  15.1 us (5%)
  between operations  13.7 us (5%)
  waiting for transfers between devices  13.2 us (4%)
  local copies, waits for them, and re-layouts  9.42 us (3%)
    pallas_call x1, Pallas kernels, gather_inputs(): pl.pallas_call(lambda *refs: gather_kernel(seq, tail, *refs), out_shape=(...  136 us
    pallas_call x1, Pallas kernels, to_owners(): pl.pallas_call(lambda *refs: owners_kernel(seq, rows, tail, *refs), out_s...  59.6 us
    ppermute x1, starting transfers between devices, head_body(): others = lax.ppermute(keys_values, 'seq', [(i, i ^ 1) for i in range(seq)])  19.3 us
    all_gather x1, waiting for transfers between devices, head_body(): out_weights = lax.all_gather(columns, 'seq', axis=1, tiled=True)  13.2 us
    dot_general x1, matrix products, head_body(): jnp.dot(normed, weights, preferred_element_type=jnp.float32)  6.92 us
    dot_general x1, matrix products, head_body(): head_total = jnp.dot(mine, out_weights, preferred_element_type=jnp.float32)  6.63 us
  transfers between devices with their start and end apart: 3, of which 1 were waited for; matrix products, arithmetic and copies ran while one was open for 12% of the time, Pallas kernels for 20%

profile of v2, /device:TPU:5, one launch (start us, length us, event | category | flops | bytes accessed | tf_op | source)
XLA Modules:
  0.0 297.3 jit_solution(8297559865141038282)
XLA Ops:
  6.5 2.1 copy.29
  8.7 1.7 copy.30.refs_1_
  10.5 136.3 %gather_inputs.1 = (bf16[1168,4096]{1,0:T(8,128)(2,1)}, bf16[4096,384]{1,0:T(8,128)(2,1)}, bf16[2048,128]{1,0:T(8,128)(2,1)}) custom-call(bf16[256,2048]{1,0:T(8,128)(2,1)} %refs_0_.1, bf16[256,3072]{1,0:T(8,128)(2,1)} %copy.30.refs_1_, bf16[1024,256]{1,0:T(8,128)(2,1)} %bitcast.20), custom_call_target="tpu_custom_call" | custom-call | tf_op jit(solution)/shard_map/gather_inputs/pallas_call | solution.py:427
  147.1 5.2 %convert_reduce_fusion = f32[1168]{0:T(1024)S(1)} fusion(bf16[1168,4096]{1,0:T(8,128)(2,1)} %get-tuple-element.8), kind=kLoop, calls=%fused_computation.1 | loop fusion | flops 9567088 | bytes 9572928 | tf_op jit(solution)/shard_map/reduce_sum | solution.py:571
  152.3 1.2 copy-done
  153.5 2.6 fusion.2
  156.2 0.2 fusion.37
  156.4 1.2 fusion.22
  157.7 6.9 %fusion.7 = f32[1168,384]{0,1:T(8,128)S(1)} fusion(bf16[4096,384]{1,0:T(8,128)(2,1)} %get-tuple-element.9, bf16[1168,4096]{1,0:T(8,128)(2,1)S(1)} %copy-done, f32[4096]{0:T(1024)S(1)} %copy-done.5, f32[4096]{0:T(1024)S(1)} %copy-done.6, f32[1168]{0:T(1024)S(1)} %add_rsqrt_fusion, f32[1168]{0:T(1024)S(1)} %broadcast_multiply_fusion), kind=kOutput, calls=%fused_computation.13 | convolution fusion | flops 3702915072 | bytes 14550144 | tf_op jit(solution)/shard_map/dot_general | solution.py:577
  164.6 0.2 multiply_subtract_fusion.1
  165.0 1.1 copy.34
  166.1 19.3 %collective-permute-start.1 = (bf16[1168,256]{1,0:T(8,128)(2,1)}, bf16[1168,256]{1,0:T(8,128)(2,1)}, u32[]{:S(2)}, u32[]{:S(2)}) collective-permute-start(bf16[1168,256]{1,0:T(8,128)(2,1)} %copy.34), channel_id=1, source_target_pairs={{0,2},{2,0},{4,6},{6,4},{8,10},{10,8},{12,14},{14,12},{16,18},{18,... | collective-permute-start | bytes 1794056 | tf_op jit(solution)/shard_map/ppermute | solution.py:590
  185.4 1.9 collective-permute-start
  187.7 0.7 slice.56
  188.6 0.6 add_compare_fusion
  189.4 0.2 fusion.13.pick_ref
  189.6 2.2 copy.35
  191.8 4.5 %fusion.54 = (f32[1168]{0:T(1024)S(1)}, f32[1168,2336]{1,0:T(8,128)S(1)}) fusion(bf16[1168,256]{0,1:T(8,128)(2,1)S(1)} %maximum_select_fusion, bf16[1168,256]{0,1:T(8,128)(2,1)} %copy.35, bf16[1168,2,128]{0,2,1:T(8,128)(2,1)S(1)} %maximum_convert_fusion, s32[2336]{0:T(1024)S(1)} %pad_add_fusion, s32[1168]{0:T(1024)S(1)} %get-tuple-element.15, ...), kind=kOutput, calls=%fused_computation.123 | convolution fusion | flops 716048256 | bytes 12525120 | tf_op jit(solution)/shard_map/dot_general | solution.py:596
  196.3 3.9 %fusion.9 = f32[1168]{0:T(1024)S(1)} fusion(f32[1168,2336]{1,0:T(8,128)S(1)} %get-tuple-element.38, f32[1168]{0:T(1024)S(1)} %get-tuple-element.37, s32[2336]{0:T(1024)S(1)} %pad_add_fusion, s32[1168]{0:T(1024)S(1)} %get-tuple-element.15, pred[2336]{0:T(1024)(128)(4,1)S(1)} %pad_add_fusion.1, pred[1168]{0:T(1024)(128)(4,1)S(1)} %get-tuple-element.18), kind=kLoop, calls=%fused_computation.14 | loop fusion | flops 16369520 | bytes 10940656 | tf_op jit(solution)/shard_map/reduce_sum | solution.py:602
  200.3 5.2 %fusion.12.refs_0_ = bf16[1168,128]{1,0:T(8,128)(2,1)} fusion(f32[1168,2336]{1,0:T(8,128)S(1)} %get-tuple-element.38, f32[1168]{0:T(1024)S(1)} %broadcast_select_fusion, f32[1168]{0:T(1024)S(1)} %get-tuple-element.37, s32[2336]{0:T(1024)S(1)} %pad_add_fusion, s32[1168]{0:T(1024)S(1)} %get-tuple-element.15, pred[2336]{0:T(1024)(128)(4,1)S(1)} %pad_add_fusion.1, ...), kind=kOutput, calls=%fused_computation.19 | convolution fusion | flops 719076864 | bytes 12435696 | tf_op jit(solution)/shard_map/dot_general | solution.py:604
  205.5 59.6 %to_owners.1 = bf16[304,2048]{1,0:T(8,128)(2,1)} custom-call(bf16[1168,128]{1,0:T(8,128)(2,1)} %fusion.12.refs_0_), custom_call_target="tpu_custom_call" | custom-call | tf_op jit(solution)/shard_map/to_owners/pallas_call | solution.py:520
  265.2 13.2 %all-gather.2.cloned.1.call-done = bf16[2048,2048]{1,0:T(8,128)(2,1)} async-done(((bf16[2048,128]{1,0:T(8,128)(2,1)}), bf16[2048,2048]{1,0:T(8,128)(2,1)}) %all-gather.2.cloned.1.call-update) | async-done | bytes 8388624 | tf_op jit(solution)/shard_map/all_gather | solution.py:569
  278.3 6.6 %fusion.14.rows_ref = bf16[304,2048]{1,0:T(8,128)(2,1)S(1)} fusion(bf16[48,2048]{1,0:T(8,128)(2,1)} %collective-permute-done, bf16[256,2048]{1,0:T(8,128)(2,1)S(1)} %copy-done.1, bf16[304,2048]{1,0:T(8,128)(2,1)} %to_owners.1, bf16[2048,2048]{1,0:T(8,128)(2,1)} %all-gather.2.cloned.1.call-done, f32[2048]{0:T(1024)S(1)} %copy-done.7, ...), kind=kOutput, calls=%fused_computation.23 | convolution fusion | flops 2555117568 | bytes 12132656 | tf_op jit(solution)/shard_map/dot_general | solution.py:608
  284.9 5.5 %merge_rows.1 = bf16[256,4,2048]{2,1,0:T(4,128)(2,1)} custom-call(bf16[1024,304]{1,0:T(8,128)(2,1)S(1)} %fusion.13.pick_ref, bf16[304,2048]{1,0:T(8,128)(2,1)S(1)} %fusion.14.rows_ref), custom_call_target="tpu_custom_call" | custom-call | tf_op jit(solution)/shard_map/merge_rows/pallas_call | solution.py:539
  (47 shorter events, 1.4 us)
Async XLA Ops:
  6.5 271.8 %all-gather.2.cloned.1.call-start = ((), (), s32[]{:S(2)}) async-start(), calls=%async_computation | async-start | bytes 8912896 | tf_op jit(solution)/shard_map/all_gather | solution.py:569
  8.7 138.1 %copy-start.3 = (s32[3]{0:T(128)S(1)}, s32[3]{0:T(128)}, u32[]{:S(2)}) copy-start(s32[3]{0:T(128)} %param.15) | copy-start | bytes 40
  8.7 138.3 %copy-start.4 = (s32[2]{0:T(128)S(1)}, s32[2]{0:T(128)}, u32[]{:S(2)}) copy-start(s32[2]{0:T(128)} %param.14) | copy-start | bytes 28
  147.1 6.4 %copy-start = (bf16[1168,4096]{1,0:T(8,128)(2,1)S(1)}, bf16[1168,4096]{1,0:T(8,128)(2,1)}, u32[]{:S(2)}) copy-start(bf16[1168,4096]{1,0:T(8,128)(2,1)} %get-tuple-element.8) | copy-start | bytes 28704772
  153.5 4.1 %copy-start.5 = (f32[4096]{0:T(1024)S(1)}, f32[4096]{0:T(1024)}, u32[]{:S(2)}) copy-start(f32[4096]{0:T(1024)} %param.10) | copy-start | bytes 49156
  153.5 4.1 %copy-start.6 = (f32[4096]{0:T(1024)S(1)}, f32[4096]{0:T(1024)}, u32[]{:S(2)}) copy-start(f32[4096]{0:T(1024)} %param.9) | copy-start | bytes 49156
  164.8 20.6 %copy-start.1 = (bf16[256,2048]{1,0:T(8,128)(2,1)S(1)}, bf16[256,2048]{1,0:T(8,128)(2,1)}, u32[]{:S(2)}) copy-start(bf16[256,2048]{1,0:T(8,128)(2,1)} %refs_0_.1) | copy-start | bytes 3145732
  166.1 23.5 %collective-permute-start.1 = (bf16[1168,256]{1,0:T(8,128)(2,1)}, bf16[1168,256]{1,0:T(8,128)(2,1)}, u32[]{:S(2)}, u32[]{:S(2)}) collective-permute-start(bf16[1168,256]{1,0:T(8,128)(2,1)} %copy.34), channel_id=1, source_target_pairs={{0,2},{2,0},{4,6},{6,4},{8,10},{10,8},{12,14},{14,12},{16,18},{18,... | collective-permute-start | bytes 1794056 | tf_op jit(solution)/shard_map/ppermute | solution.py:590
  185.4 79.8 %collective-permute-start = (bf16[48,2048]{1,0:T(8,128)(2,1)S(1)}, bf16[48,2048]{1,0:T(8,128)(2,1)}, u32[]{:S(2)}, u32[]{:S(2)}) collective-permute-start(bf16[48,2048]{1,0:T(8,128)(2,1)S(1)} %slice.57), channel_id=1, source_target_pairs={{2,0},{4,2},{6,4},{8,6},{10,8},{12,10},{14,12},{16,14},{18,16},{20... | collective-permute-start | bytes 589832 | tf_op jit(solution)/shard_map/ppermute | solution.py:17
  196.3 3.9 %copy-start.2 = (bf16[1168,256]{0,1:T(8,128)(2,1)S(1)}, bf16[1168,256]{0,1:T(8,128)(2,1)}, u32[]{:S(2)}) copy-start(bf16[1168,256]{0,1:T(8,128)(2,1)} %copy.35) | copy-start | bytes 1794052
  200.2 78.1 %copy-start.7 = (f32[2048]{0:T(1024)S(1)}, f32[2048]{0:T(1024)}, u32[]{:S(2)}) copy-start(f32[2048]{0:T(1024)} %param.13) | copy-start | bytes 24580
Sparse Core Ops, SparseCore 0:
  146.9 131.4 all-gather.1

commit v3 on v2

--- a/solution.py
+++ b/solution.py
@@ -338,33 +338,19 @@
 
     send_slabs(False)
 
-    out_rows, out_columns = o_ref.shape
-    piece = out_columns // 2
-    goes = [(2 * lax.rem(s, pairs) + u, s // pairs) for u in range(2)]
-    comes = pairs * t + s // 2
-
-    def column_block(u, into, device):
-        return pltpu.make_async_remote_copy(
-            src_ref=o_ref.at[:, pl.ds(piece * u, piece)],
-            dst_ref=og_ref.at[pl.ds(pl.multiple_of(out_rows * into, 128), out_rows), :],
-            send_sem=osend.at[u],
-            recv_sem=orecv.at[into],
-            device_id=device,
-            device_id_type=MESH,
-        )
-
-    def column_blocks(remote_act, local_act):
-        for u in range(2):
-            to_s, to_t = goes[u]
-            stays = jnp.logical_and(to_s == s, to_t == t)
-            copy = column_block(u, t, (to_s, to_t))
-            local = pltpu.make_async_copy(
-                o_ref.at[:, pl.ds(piece * u, piece)],
-                og_ref.at[pl.ds(pl.multiple_of(out_rows * t, 128), out_rows), :],
-                osend.at[u],
-            )
-            pl.when(jnp.logical_not(stays))(lambda: remote_act(copy))
-            pl.when(stays)(lambda: local_act(local))
+    goes_s, goes_t = 2 * lax.rem(s, pairs) + t, s // pairs
+    comes_s, comes_t = pairs * t + s // 2, lax.rem(s, 2)
+    out_sends = pltpu.make_async_remote_copy(
+        src_ref=o_ref,
+        dst_ref=og_ref,
+        send_sem=osend,
+        recv_sem=orecv,
+        device_id=(goes_s, goes_t),
+        device_id_type=MESH,
+    )
+    out_stays = pltpu.make_async_copy(o_ref, og_ref, osend)
+    stays = jnp.logical_and(goes_s == s, goes_t == t)
+    stayed = jnp.logical_and(comes_s == s, comes_t == t)
 
     def onward(source, step):
         part = wg_ref.at[pl.ds(pl.multiple_of(source * depth, 128), depth), :]
@@ -390,7 +376,8 @@
         send(near, move(zp, y, 1 - t, 1, 2, (y_side, t)))
 
     send_slabs(True)
-    column_blocks(lambda copy: copy.start(), lambda local: local.start())
+    pl.when(jnp.logical_not(stays))(out_sends.start)
+    pl.when(stays)(out_stays.start)
     mine.wait()
     onward(s, 0).start()
     for step in range(1, pairs):
@@ -412,10 +399,9 @@
         if step:
             to = pair_at(step)
             slab(s, to, wsend.at[step], wrecv.at[step], (2 * to + c, t)).wait_send()
-    column_blocks(lambda copy: copy.wait_send(), lambda local: local.wait())
-    for into in range(2):
-        remote = jnp.logical_or(comes != s, into != t)
-        pl.when(remote)(column_block(0, into, (core_side, t)).wait_recv)
+    pl.when(jnp.logical_not(stays))(out_sends.wait_send)
+    pl.when(stays)(out_stays.wait)
+    pl.when(jnp.logical_not(stayed))(out_sends.wait_recv)
     for cond, copy in pending:
         when(cond, copy.wait_send)
 
@@ -429,9 +415,7 @@
         out_shape=(
             jax.ShapeDtypeStruct((4 * rows + tail, 2 * width), tokens.dtype),
             jax.ShapeDtypeStruct((weights.shape[0] * seq, head_width), weights.dtype),
-            jax.ShapeDtypeStruct(
-                (2 * out_weights.shape[0], out_weights.shape[1] // 2), weights.dtype
-            ),
+            jax.ShapeDtypeStruct(out_weights.shape, out_weights.dtype),
         ),
         in_specs=[pl.BlockSpec(memory_space=pl.ANY)] * 3,
         out_specs=[pl.BlockSpec(memory_space=pl.ANY)] * 3,
@@ -444,8 +428,8 @@
             dma((seq // 2,)),
             dma((seq // 2,)),
             dma((seq // 2,)),
-            dma((2,)),
-            dma((2,)),
+            dma,
+            dma,
         ],
         compiler_params=pltpu.CompilerParams(collective_id=0, has_side_effects=True),
         name="gather_inputs",
@@ -528,6 +512,32 @@
     )(attended)
 
 
+def project_kernel(mine_ref, w_ref, tokens_ref, scale_ref, real_ref, out_ref):
+    total = jnp.dot(mine_ref[...], w_ref[0], preferred_element_type=jnp.float32)
+    layer_out = tokens_ref[...].astype(jnp.float32) + scale_ref[...] * total
+    out_ref[...] = jnp.where(real_ref[...] > 0, layer_out, 0.0).astype(out_ref.dtype)
+
+
+def project(mine, out_weights, tokens, scale, real):
+    count, depth = mine.shape
+    blocks, _, part = out_weights.shape
+    return pl.pallas_call(
+        project_kernel,
+        grid=(blocks,),
+        out_shape=jax.ShapeDtypeStruct(tokens.shape, tokens.dtype),
+        in_specs=[
+            pl.BlockSpec((count, depth), lambda i: (0, 0)),
+            pl.BlockSpec((1, depth, part), lambda i: (i, 0, 0)),
+            pl.BlockSpec((count, part), lambda i: (0, i)),
+            pl.BlockSpec((1, part), lambda i: (0, i)),
+            pl.BlockSpec((count, 1), lambda i: (0, 0)),
+        ],
+        out_specs=pl.BlockSpec((count, part), lambda i: (0, i)),
+        compiler_params=pltpu.CompilerParams(vmem_limit_bytes=56 * 1024 * 1024),
+        name="project",
+    )(mine, out_weights, tokens, scale, real)
+
+
 def merge_kernel(pick_ref, rows_ref, out_ref):
     count, four, width = out_ref.shape
     picked = jnp.dot(pick_ref[...], rows_ref[...], preferred_element_type=jnp.float32)
@@ -566,7 +576,8 @@
         seq,
         tail,
     )
-    out_weights = lax.all_gather(columns, "seq", axis=1, tiled=True)
+    out_weights = lax.all_gather(columns, "seq", axis=0, tiled=True)
+    out_weights = out_weights.reshape(seq // 2, 2 * columns.shape[0], columns.shape[1])
     widened = gathered.astype(jnp.float32)
     average = jnp.mean(widened, axis=-1, keepdims=True)
     spread_sq = jnp.mean(jnp.square(widened - average), axis=-1, keepdims=True)
@@ -605,13 +616,10 @@
     attended = jnp.where(inside[:, None], attended, 0.0).astype(jnp.bfloat16)
 
     mine = to_owners(attended, seq, rows, tail)
-    head_total = jnp.dot(mine, out_weights, preferred_element_type=jnp.float32)
-    extended_tokens = jnp.concatenate([tokens, token_halo], axis=0).astype(jnp.float32)
-    extended = (extended_tokens + layer_scale * head_total).astype(jnp.bfloat16)
+    extended_tokens = jnp.concatenate([tokens, token_halo], axis=0)
     extended_ids = s * rows + jnp.arange(rows + HALO, dtype=jnp.int32)
-    extended = jnp.where(
-        (extended_ids < offsets[-1])[:, None], extended, jnp.zeros_like(extended)
-    )
+    real = (extended_ids < offsets[-1]).astype(jnp.int32)[:, None]
+    extended = project(mine, out_weights, extended_tokens, layer_scale[None, :], real)
 
     local_ids = jnp.arange(rows, dtype=jnp.int32)
     _, _, is_patch, grid_row, grid_col, grid_side = layout_rows(

time: 298 us -> 296 us (level)
  matrix products: 23.3 us -> 15.6 us
  other arithmetic: 15.1 us -> 18.8 us
    ppermute x1, waiting for transfers between devices: 0.01 us -> 11.1 us  [from_behind(): return lax.ppermute(shard, axis, pairs)]
    pallas_call x1, Pallas kernels: 59.6 us -> 48.7 us  [to_owners(): pl.pallas_call(lambda *refs: owners_kernel(seq, rows, tail, *refs), out_s...]
    all_gather x1, waiting for transfers between devices: 13.2 us -> 2.56 us  [head_body(): out_weights = lax.all_gather(columns, 'seq', axis=0, tiled=True)]
    pallas_call x0 -> x1, Pallas kernels: none -> 9.41 us  [project(): pl.pallas_call(project_kernel, grid=(blocks,), out_shape=jax.ShapeDtypeSt...]
    dot_general x1 -> x0, matrix products: 6.63 us -> none  [head_body(): head_total = jnp.dot(mine, out_weights, preferred_element_type=jnp.float32)]
  transfers between devices with their start and end apart: 3 -> 3, of which waited for: 1 -> 2; matrix products, arithmetic and copies ran while one was open for 12% -> 13% of each run, Pallas kernels for 20% -> 17%
where the time goes in v3:
time: 296 us; the launch traced here: 294 us
  Pallas kernels  200 us (68%)
  starting transfers between devices  21.5 us (7%)
  other arithmetic  18.8 us (6%)
  matrix products  15.6 us (5%)
  between operations  13.8 us (5%)
  waiting for transfers between devices  13.6 us (5%)
  local copies, waits for them, and re-layouts  10.9 us (4%)
    pallas_call x1, Pallas kernels, gather_inputs(): pl.pallas_call(lambda *refs: gather_kernel(seq, tail, *refs), out_shape=(...  136 us
    pallas_call x1, Pallas kernels, to_owners(): pl.pallas_call(lambda *refs: owners_kernel(seq, rows, tail, *refs), out_s...  48.7 us
    ppermute x1, starting transfers between devices, head_body(): others = lax.ppermute(keys_values, 'seq', [(i, i ^ 1) for i in range(seq)])  19.5 us
    ppermute x1, waiting for transfers between devices, from_behind(): return lax.ppermute(shard, axis, pairs)  11.1 us
    pallas_call x1, Pallas kernels, project(): pl.pallas_call(project_kernel, grid=(blocks,), out_shape=jax.ShapeDtypeSt...  9.41 us
    dot_general x1, matrix products, head_body(): jnp.dot(normed, weights, preferred_element_type=jnp.float32)  7.06 us
  transfers between devices with their start and end apart: 3, of which 2 were waited for; matrix products, arithmetic and copies ran while one was open for 13% of the time, Pallas kernels for 17%

profile of v3, /device:TPU:5, one launch (start us, length us, event | category | flops | bytes accessed | tf_op | source)
XLA Modules:
  0.0 293.7 jit_solution(2575788406950444854)
XLA Ops:
  6.5 2.1 copy.37
  8.7 1.7 copy.38.refs_1_
  10.5 136.0 %gather_inputs.1 = (bf16[1168,4096]{1,0:T(8,128)(2,1)}, bf16[4096,384]{1,0:T(8,128)(2,1)}, bf16[1024,256]{1,0:T(8,128)(2,1)}) custom-call(bf16[256,2048]{1,0:T(8,128)(2,1)} %refs_0_.1, bf16[256,3072]{1,0:T(8,128)(2,1)} %copy.38.refs_1_, bf16[1024,256]{1,0:T(8,128)(2,1)} %bitcast.21), custom_call_target="tpu_custom_call" | custom-call | tf_op jit(solution)/shard_map/gather_inputs/pallas_call | solution.py:413
  147.2 5.2 %convert_reduce_fusion = f32[1168]{0:T(1024)S(1)} fusion(bf16[1168,4096]{1,0:T(8,128)(2,1)} %get-tuple-element.8), kind=kLoop, calls=%fused_computation.1 | loop fusion | flops 9567088 | bytes 9572928 | tf_op jit(solution)/shard_map/reduce_sum | solution.py:582
  152.4 1.2 copy-done.1
  153.7 2.6 fusion.2
  156.5 1.2 fusion.21
  157.8 7.1 %fusion.7 = f32[1168,384]{0,1:T(8,128)S(1)} fusion(bf16[4096,384]{1,0:T(8,128)(2,1)} %get-tuple-element.9, bf16[1168,4096]{1,0:T(8,128)(2,1)S(1)} %copy-done.1, f32[4096]{0:T(1024)S(1)} %copy-done.14, f32[4096]{0:T(1024)S(1)} %copy-done.15, f32[1168]{0:T(1024)S(1)} %add_rsqrt_fusion, f32[1168]{0:T(1024)S(1)} %broadcast_multiply_fusion), kind=kOutput, calls=%fused_computation.13 | convolution fusion | flops 3702915072 | bytes 14550144 | tf_op jit(solution)/shard_map/dot_general | solution.py:588
  165.4 1.1 copy.42
  166.4 19.5 %collective-permute-start = (bf16[1168,256]{1,0:T(8,128)(2,1)}, bf16[1168,256]{1,0:T(8,128)(2,1)}, u32[]{:S(2)}, u32[]{:S(2)}) collective-permute-start(bf16[1168,256]{1,0:T(8,128)(2,1)} %copy.42), channel_id=1, source_target_pairs={{0,2},{2,0},{4,6},{6,4},{8,10},{10,8},{12,14},{14,12},{16,18},{18,... | collective-permute-start | bytes 1794056 | tf_op jit(solution)/shard_map/ppermute | solution.py:601
  186.0 1.9 collective-permute-start.1
  190.4 1.3 fusion.22.real_ref
  192.6 0.9 fusion.13.pick_ref
  193.5 11.1 %collective-permute-done.1 = bf16[48,2048]{1,0:T(8,128)(2,1)S(1)} collective-permute-done((bf16[48,2048]{1,0:T(8,128)(2,1)S(1)}, bf16[48,2048]{1,0:T(8,128)(2,1)S(1)}, u32[]{:S(2)}, u32[]{:S(2)}) %collective-permute-start.1) | collective-permute-done | bytes 196640 | tf_op jit(solution)/shard_map/ppermute | solution.py:17
  204.5 1.1 pad_maximum_fusion.tokens_ref
  205.6 1.3 copy.43
  207.0 3.5 %fusion.54 = (f32[1168]{0:T(1024)S(1)}, f32[1168,2336]{1,0:T(8,128)S(1)}) fusion(bf16[1168,256]{0,1:T(8,128)(2,1)S(1)} %maximum_select_fusion, bf16[1168,256]{0,1:T(8,128)(2,1)S(1)} %copy.43, bf16[1168,2,128]{0,2,1:T(8,128)(2,1)S(1)} %maximum_convert_fusion, s32[2336]{0:T(1024)S(1)} %copy-done.5, s32[1168]{0:T(1024)S(1)} %get-tuple-element.15, ...), kind=kOutput, calls=%fused_computation.122 | convolution fusion | flops 716048256 | bytes 12582464 | tf_op jit(solution)/shard_map/dot_general | solution.py:607
  210.5 3.9 %fusion.9 = f32[1168]{0:T(1024)S(1)} fusion(f32[1168,2336]{1,0:T(8,128)S(1)} %get-tuple-element.38, f32[1168]{0:T(1024)S(1)} %get-tuple-element.37, s32[2336]{0:T(1024)S(1)} %copy-done.5, s32[1168]{0:T(1024)S(1)} %get-tuple-element.15, pred[2336]{0:T(1024)(128)(4,1)S(1)} %pad_add_fusion.1, pred[1168]{0:T(1024)(128)(4,1)S(1)} %copy-done.4), kind=kLoop, calls=%fused_computation.14 | loop fusion | flops 16369520 | bytes 10940656 | tf_op jit(solution)/shard_map/reduce_sum | solution.py:613
  214.4 5.0 %fusion.12.refs_0_ = bf16[1168,128]{1,0:T(8,128)(2,1)} fusion(f32[1168,2336]{1,0:T(8,128)S(1)} %get-tuple-element.38, f32[1168]{0:T(1024)S(1)} %broadcast_select_fusion, f32[1168]{0:T(1024)S(1)} %get-tuple-element.37, s32[2336]{0:T(1024)S(1)} %copy-done.5, s32[1168]{0:T(1024)S(1)} %get-tuple-element.15, pred[2336]{0:T(1024)(128)(4,1)S(1)} %pad_add_fusion.1, ...), kind=kOutput, calls=%fused_computation.17 | convolution fusion | flops 719076864 | bytes 12435696 | tf_op jit(solution)/shard_map/dot_general | solution.py:615
  219.4 48.7 %to_owners.1.mine_ref = bf16[304,2048]{1,0:T(8,128)(2,1)} custom-call(bf16[1168,128]{1,0:T(8,128)(2,1)} %fusion.12.refs_0_), custom_call_target="tpu_custom_call" | custom-call | tf_op jit(solution)/shard_map/to_owners/pallas_call | solution.py:504
  268.1 2.6 all-gather.2.cloned.1.call-done
  270.7 9.4 %project.1.rows_ref = bf16[304,2048]{1,0:T(8,128)(2,1)} custom-call(bf16[304,2048]{1,0:T(8,128)(2,1)} %to_owners.1.mine_ref, bf16[8,2048,256]{2,1,0:T(8,128)(2,1)} %bitcast.17, bf16[304,2048]{1,0:T(8,128)(2,1)} %pad_maximum_fusion.tokens_ref, f32[1,2048]{1,0:T(1,128)} %bitcast.23, s32[304,1]{1,0:T(8,128)} %fusion.22.real_ref), custom_call_target="tpu_custom_call" | custom-call | tf_op jit(solution)/shard_map/project/pallas_call | solution.py:524
  280.1 1.3 copy-done
  281.4 5.5 %merge_rows.1 = bf16[256,4,2048]{2,1,0:T(4,128)(2,1)} custom-call(bf16[1024,304]{1,0:T(8,128)(2,1)S(1)} %fusion.13.pick_ref, bf16[304,2048]{1,0:T(8,128)(2,1)S(1)} %copy-done), custom_call_target="tpu_custom_call" | custom-call | tf_op jit(solution)/shard_map/merge_rows/pallas_call | solution.py:549
  (64 shorter events, 4.8 us)
Async XLA Ops:
  6.5 264.1 %all-gather.2.cloned.1.call-start = ((), (), s32[]{:S(2)}) async-start(), calls=%async_computation | async-start | bytes 8912896 | tf_op jit(solution)/shard_map/all_gather | solution.py:579
  8.7 137.8 %copy-start.10 = (s32[3]{0:T(128)S(1)}, s32[3]{0:T(128)}, u32[]{:S(2)}) copy-start(s32[3]{0:T(128)} %param.15) | copy-start | bytes 40
  8.7 138.4 %copy-start.12 = (s32[2]{0:T(128)S(1)}, s32[2]{0:T(128)}, u32[]{:S(2)}) copy-start(s32[2]{0:T(128)} %param.14) | copy-start | bytes 28
  146.6 0.6 copy-start.6
  146.6 5.9 %copy-start.8 = (s32[2]{0:T(128)}, s32[2]{0:T(128)S(1)}, u32[]{:S(2)}) copy-start(s32[2]{0:T(128)S(1)} %get-tuple-element.36) | copy-start | bytes 28
  147.2 6.4 %copy-start.1 = (bf16[1168,4096]{1,0:T(8,128)(2,1)S(1)}, bf16[1168,4096]{1,0:T(8,128)(2,1)}, u32[]{:S(2)}) copy-start(bf16[1168,4096]{1,0:T(8,128)(2,1)} %get-tuple-element.8) | copy-start | bytes 28704772
  153.7 4.1 %copy-start.14 = (f32[4096]{0:T(1024)S(1)}, f32[4096]{0:T(1024)}, u32[]{:S(2)}) copy-start(f32[4096]{0:T(1024)} %param.10) | copy-start | bytes 49156
  153.7 4.1 %copy-start.15 = (f32[4096]{0:T(1024)S(1)}, f32[4096]{0:T(1024)}, u32[]{:S(2)}) copy-start(f32[4096]{0:T(1024)} %param.9) | copy-start | bytes 49156
  156.3 8.9 %copy-start.3 = (pred[1168]{0:T(1024)(128)(4,1)}, pred[1168]{0:T(1024)(128)(4,1)S(1)}, u32[]{:S(2)}) copy-start(pred[1168]{0:T(1024)(128)(4,1)S(1)} %get-tuple-element.18) | copy-start | bytes 3508
  165.0 20.9 %copy-start.2 = (bf16[256,2048]{1,0:T(8,128)(2,1)S(1)}, bf16[256,2048]{1,0:T(8,128)(2,1)}, u32[]{:S(2)}) copy-start(bf16[256,2048]{1,0:T(8,128)(2,1)} %refs_0_.1) | copy-start | bytes 3145732
  165.0 22.9 %copy-start.11 = (s32[3]{0:T(128)S(1)}, s32[3]{0:T(128)}, u32[]{:S(2)}) copy-start(s32[3]{0:T(128)} %param.15) | copy-start | bytes 40
  165.1 23.5 %copy-start.7 = (s32[2]{0:T(128)S(1)}, s32[2]{0:T(128)}, u32[]{:S(2)}) copy-start(s32[2]{0:T(128)} %copy-done.6) | copy-start | bytes 28
  165.1 23.5 %copy-start.9 = (s32[2]{0:T(128)S(1)}, s32[2]{0:T(128)}, u32[]{:S(2)}) copy-start(s32[2]{0:T(128)} %copy-done.8) | copy-start | bytes 28
  165.1 23.5 %copy-start.13 = (s32[2]{0:T(128)S(1)}, s32[2]{0:T(128)}, u32[]{:S(2)}) copy-start(s32[2]{0:T(128)} %param.14) | copy-start | bytes 28
  166.4 39.2 %collective-permute-start = (bf16[1168,256]{1,0:T(8,128)(2,1)}, bf16[1168,256]{1,0:T(8,128)(2,1)}, u32[]{:S(2)}, u32[]{:S(2)}) collective-permute-start(bf16[1168,256]{1,0:T(8,128)(2,1)} %copy.42), channel_id=1, source_target_pairs={{0,2},{2,0},{4,6},{6,4},{8,10},{10,8},{12,14},{14,12},{16,18},{18,... | collective-permute-start | bytes 1794056 | tf_op jit(solution)/shard_map/ppermute | solution.py:601
  186.0 18.5 %collective-permute-start.1 = (bf16[48,2048]{1,0:T(8,128)(2,1)S(1)}, bf16[48,2048]{1,0:T(8,128)(2,1)S(1)}, u32[]{:S(2)}, u32[]{:S(2)}) collective-permute-start(bf16[48,2048]{1,0:T(8,128)(2,1)S(1)} %slice.65), channel_id=1, source_target_pairs={{2,0},{4,2},{6,4},{8,6},{10,8},{12,10},{14,12},{16,14},{18,16},{20... | collective-permute-start | bytes 589832 | tf_op jit(solution)/shard_map/ppermute | solution.py:17
  191.7 15.2 %copy-start.4 = (pred[1168]{0:T(1024)(128)(4,1)S(1)}, pred[1168]{0:T(1024)(128)(4,1)}, u32[]{:S(2)}) copy-start(pred[1168]{0:T(1024)(128)(4,1)} %copy-done.3) | copy-start | bytes 3508
  204.5 2.4 copy-start.5
  280.1 1.3 copy-start
Sparse Core Ops, SparseCore 0:
  146.6 124.0 all-gather.1
